TPU v7x, 128 devices: a whole 4x4x4 slice. The times are simulated.
128 devices in a mesh: dp: 2 (over core), context: 16 (over y, x), tensor: 4 (over z).
Axes of the slice: x: 4, y: 4, z: 4, core: 2. Of those that a mesh axis runs over, the one named last changes fastest.
Arguments:
- ids: int32 [16384], P(('dp', 'context', 'tensor')), parts along dimension 0, may hold values from 65 to 84, as said below
- block_order: int32 [64], P('dp'), parts along dimension 0, may hold values from 0 to 31, each once
- embed: bfloat16 [512, 4096], replicated, may hold values from -6 to 6
- mix_gain: float32 [4096], replicated, may hold values from 0.5 to 2
- in_proj: bfloat16 [3, 4096, 2048], P(None, None, 'tensor'), may hold values from -0.09375 to 0.09375
- short_filter: float32 [3, 3, 2048], P(None, None, 'tensor'), may hold values from -1 to 1
- long_filter: float32 [128, 128], P('tensor'), as said below
- conv_skip: float32 [2048], P('tensor'), may hold values from -1 to 1
- hyena_out: bfloat16 [2048, 4096], P('tensor'), may hold values from -0.125 to 0.125
- attn_gain: float32 [4096], replicated, may hold values from 0.5 to 2
- qkv_proj: bfloat16 [3, 4096, 2048], P(None, None, 'tensor'), as said below
- attn_out: bfloat16 [2048, 4096], P('tensor'), may hold values from -0.5 to 0.5
Outputs:
- stream_out: float32 [16384, 4096], P(('dp', 'context', 'tensor')), parts along dimension 0
There are 2 independent parts, one for each index of `dp`. A program takes and returns all parts, laid end to end along the dimension named above; an argument that names none is the same for every part. Nothing has to cross between parts.
Inputs may be any that keep to these rules, and one draw needn't show every extreme that they name: `ids`: every id is the code of a base: 65, 67, 71 or 84. `block_order`: every block lies in exactly one slot. `long_filter`: real-valued filter taps. `qkv_proj`: real-valued projection weights.
All inputs are finite; a program needn't handle non-finite values.
Results may differ from a plain program's by a relative error of at most 0.01.
Values may be sent and summed in bfloat16 or wider, within the bound.
A program may use at most 192 MiB of HBM per device.

v0:
```python
import math

import jax
import jax.numpy as jnp
from jax import lax
from jax.sharding import PartitionSpec as P

HD = 128
GROUP_CH = 16


EPS = 1e-06
THETA = 1000000.0
NEG_FILL = -1e30


def rms_scale(row_data, gain_vec):
    values = row_data.astype(jnp.float32)
    factor = lax.rsqrt(jnp.mean(values * values, axis=-1, keepdims=True) + EPS)
    return (values * factor * gain_vec).astype(jnp.bfloat16)


def toeplitz(long_filter):
    filter_len = long_filter.shape[1]
    tap_lag = (
        jnp.arange(filter_len, dtype=jnp.int32)[:, None]
        - jnp.arange(filter_len, dtype=jnp.int32)[None, :]
    )
    near_taps = jnp.take(long_filter, jnp.clip(tap_lag, 0, filter_len - 1), axis=1)
    far_taps = jnp.take(long_filter, jnp.clip(tap_lag + filter_len, 0, filter_len - 1), axis=1)
    near_taps = jnp.where(tap_lag[None] >= 0, near_taps, jnp.zeros_like(near_taps))
    far_taps = jnp.where(tap_lag[None] < 0, far_taps, jnp.zeros_like(far_taps))
    return (near_taps, far_taps)


def long_conv(padded, long_filter, group_width):
    filter_len = long_filter.shape[1]
    near_taps, far_taps = toeplitz(long_filter)
    row_total = padded.shape[0]
    chan_total = padded.shape[1]
    blocks = padded.reshape(
        row_total // filter_len, filter_len, chan_total // group_width, group_width
    )
    current_part = jnp.einsum(
        "grs,bsgc->brgc", near_taps, blocks[1:], precision=lax.Precision.HIGHEST
    )
    before = jnp.einsum("grs,bsgc->brgc", far_taps, blocks[:-1], precision=lax.Precision.HIGHEST)
    return (current_part + before).reshape(row_total - filter_len, chan_total)


def short_conv(padded_rows, short_filter, out_len):
    taps = short_filter.shape[1]
    result = jnp.zeros((padded_rows.shape[0], out_len, padded_rows.shape[2]), jnp.float32)
    for tap_at in range(taps):
        offset = taps - 1 - tap_at
        result = (
            result + short_filter[:, tap_at][:, None, :] * padded_rows[:, offset : offset + out_len]
        )
    return result


def rotate(values, positions, head_dim):
    half_dim = head_dim // 2
    inverse_freq = THETA ** (-(2.0 * jnp.arange(half_dim, dtype=jnp.float32)) / head_dim)
    angles = positions.astype(jnp.float32)[:, None] * inverse_freq[None, :]
    cosine_part = jnp.cos(angles)[:, None, :]
    sine_part = jnp.sin(angles)[:, None, :]
    lower_half = values[..., :half_dim]
    upper_half = values[..., half_dim:]
    return jnp.concatenate(
        [
            lower_half * cosine_part - upper_half * sine_part,
            upper_half * cosine_part + lower_half * sine_part,
        ],
        axis=-1,
    )


def body(
    ids,
    block_order,
    embed,
    mix_gain,
    in_proj,
    short_filter,
    long_filter,
    conv_skip,
    hyena_out,
    attn_gain,
    qkv_proj,
    attn_out,
):
    tok_rows = ids.shape[0]
    tensor_count = lax.axis_size("tensor")
    context_count = lax.axis_size("context")
    ctx_rows = tok_rows * tensor_count
    block_rows = ctx_rows // 2
    filter_len = long_filter.shape[1]
    short_len = short_filter.shape[1]
    halo_len = filter_len + short_len - 2
    chan_local = in_proj.shape[2]
    context_at = lax.axis_index("context")
    vocab_ids = jnp.arange(embed.shape[0], dtype=jnp.int32)
    chosen = (ids[:, None] == vocab_ids[None, :]).astype(jnp.bfloat16)
    embedded = jnp.dot(chosen, embed, preferred_element_type=jnp.float32).astype(jnp.bfloat16)
    embedded_all = lax.all_gather(embedded, "tensor", axis=0, tiled=True)
    mixed_in = rms_scale(embedded_all, mix_gain)
    projected = jnp.einsum(
        "rd,jdc->jrc", mixed_in, in_proj, preferred_element_type=jnp.float32
    ).astype(jnp.bfloat16)
    slot_ids = jnp.arange(2 * context_count, dtype=jnp.int32)
    slot_pair = 2 * context_at + jnp.arange(2, dtype=jnp.int32)
    owned_blocks = jnp.sum(
        jnp.where(slot_ids[None, :] == slot_pair[:, None], block_order[None, :], 0), axis=1
    )
    local_pos = (
        owned_blocks[:, None] * block_rows + jnp.arange(block_rows, dtype=jnp.int32)[None, :]
    ).reshape(ctx_rows)
    tail_rows = jnp.stack(
        [projected[:, block_rows - halo_len : block_rows], projected[:, ctx_rows - halo_len :]]
    )
    all_tails = lax.all_gather(tail_rows, "context", axis=0, tiled=True)
    out_len = filter_len - 1 + block_rows
    pieces = []
    for block_at in range(2):
        holder_hit = (block_order == owned_blocks[block_at] - 1).astype(jnp.bfloat16)
        before_rows = jnp.einsum(
            "s,sjrc->jrc", holder_hit, all_tails, preferred_element_type=jnp.float32
        )
        own_rows = projected[:, block_at * block_rows : (block_at + 1) * block_rows].astype(
            jnp.float32
        )
        extended = jnp.concatenate([before_rows, own_rows], axis=1)
        filtered = short_conv(extended, short_filter, out_len)
        gated_rows = filtered[1] * filtered[2]
        padded = jnp.concatenate([jnp.zeros((1, chan_local), jnp.float32), gated_rows], axis=0)
        long_mix = long_conv(padded, long_filter, GROUP_CH)
        own_gate = gated_rows[filter_len - 1 :]
        pieces.append(
            (filtered[0, filter_len - 1 :] * (long_mix + conv_skip * own_gate)).astype(jnp.bfloat16)
        )
    hyena_mix = jnp.concatenate(pieces, axis=0)
    hyena_own = lax.psum_scatter(
        jnp.dot(hyena_mix, hyena_out, preferred_element_type=jnp.float32),
        "tensor",
        scatter_dimension=0,
        tiled=True,
    )
    stream_own = embedded.astype(jnp.float32) + hyena_own
    stream_all = lax.all_gather(stream_own, "tensor", axis=0, tiled=True)
    attn_in = rms_scale(stream_all, attn_gain)
    projections = jnp.einsum("rd,jdf->jrf", attn_in, qkv_proj, preferred_element_type=jnp.float32)
    local_heads = projections.shape[2] // HD
    shaped = projections.reshape(3, ctx_rows, local_heads, HD)
    queries = rotate(shaped[0], local_pos, HD).astype(jnp.bfloat16)
    keys_flat = (
        rotate(shaped[1], local_pos, HD).astype(jnp.bfloat16).reshape(ctx_rows, local_heads * HD)
    )
    values_flat = shaped[2].astype(jnp.bfloat16).reshape(ctx_rows, local_heads * HD)
    score_scale = HD ** (-0.5)
    start_state = (
        jnp.full((2, block_rows, local_heads), NEG_FILL, jnp.float32),
        jnp.zeros((2, block_rows, local_heads), jnp.float32),
        jnp.zeros((2, block_rows, local_heads, HD), jnp.float32),
    )
    key_piece = lax.all_gather(keys_flat, "context", axis=0, tiled=True)
    value_piece = lax.all_gather(values_flat, "context", axis=0, tiled=True)
    piece_len = key_piece.shape[0]
    sub_len = math.gcd(piece_len, 512)

    def attend_sub(sub_index, carried):
        key_block = lax.dynamic_slice_in_dim(key_piece, sub_index * sub_len, sub_len, 0).reshape(
            sub_len, local_heads, HD
        )
        value_block = lax.dynamic_slice_in_dim(
            value_piece, sub_index * sub_len, sub_len, 0
        ).reshape(sub_len, local_heads, HD)
        row_ids = sub_index * sub_len + jnp.arange(sub_len, dtype=jnp.int32)
        holder = row_ids // block_rows
        key_pos = (
            jnp.sum(
                jnp.where(holder[:, None] == slot_ids[None, :], block_order[None, :], 0), axis=1
            )
            * block_rows
            + row_ids % block_rows
        )
        top_all, sums_all, weighted_all = carried
        outputs = []
        for block_at in range(2):
            query_rows = queries[block_at * block_rows : (block_at + 1) * block_rows]
            query_pos = local_pos[block_at * block_rows : (block_at + 1) * block_rows]
            top_score = top_all[block_at]
            weight_sum = sums_all[block_at]
            weighted = weighted_all[block_at]
            scores = (
                jnp.einsum(
                    "qhd,khd->qhk", query_rows, key_block, preferred_element_type=jnp.float32
                )
                * score_scale
            )
            visible = key_pos[None, None, :] <= query_pos[:, None, None]
            scores = jnp.where(visible, scores, NEG_FILL)
            new_top = jnp.maximum(top_score, jnp.max(scores, axis=-1))
            rescale = jnp.exp(top_score - new_top)
            weights = jnp.where(visible, jnp.exp(scores - new_top[..., None]), 0.0)
            weight_sum = weight_sum * rescale + jnp.sum(weights, axis=-1)
            weighted = weighted * rescale[..., None] + jnp.einsum(
                "qhk,khd->qhd",
                weights.astype(jnp.bfloat16),
                value_block,
                preferred_element_type=jnp.float32,
            )
            result = (new_top, weight_sum, weighted)
            outputs.append(result)
        return tuple((jnp.stack([entry[field] for entry in outputs]) for field in range(3)))

    top_final, sums_final, weighted_final = lax.fori_loop(
        0, piece_len // sub_len, attend_sub, start_state
    )
    attended = (
        (weighted_final / sums_final[..., None])
        .astype(jnp.bfloat16)
        .reshape(ctx_rows, local_heads * HD)
    )
    attn_own = lax.psum_scatter(
        jnp.dot(attended, attn_out, preferred_element_type=jnp.float32).astype(jnp.bfloat16),
        "tensor",
        scatter_dimension=0,
        tiled=True,
    ).astype(jnp.float32)
    return stream_own + attn_own


def solution(mesh):
    placed = (
        P(("dp", "context", "tensor")),
        P("dp"),
        P(),
        P(),
        P(None, None, "tensor"),
        P(None, None, "tensor"),
        P("tensor", None),
        P("tensor"),
        P("tensor", None),
        P(),
        P(None, None, "tensor"),
        P("tensor", None),
    )
    return jax.shard_map(
        body,
        mesh=mesh,
        in_specs=placed,
        out_specs=P(("dp", "context", "tensor"), None),
        check_vma=False,
    )
```

profile of v0, /device:TPU:1, one launch (start us, length us, event | category | flops | bytes accessed | tf_op | source)
XLA Modules:
  0.0 769.8 jit_solution(17294564735795966699)
XLA Ops:
  6.5 3.9 convolution_convert_fusion.1
  10.5 51.8 %all-gather.7.cloned.1.call-done = bf16[512,4096]{1,0:T(8,128)(2,1)} async-done(((bf16[128,4096]{1,0:T(8,128)(2,1)}), bf16[512,4096]{1,0:T(8,128)(2,1)}) %all-gather.7.cloned.1.call-update) | async-done | bytes 4194320 | tf_op jit(solution)/shard_map/all_gather | solution.py:106
  62.3 3.2 fusion.42
  65.8 9.9 %fusion.83 = bf16[3,512,512]{2,1,0:T(8,128)(2,1)S(1)} fusion(bf16[3,4096,512]{2,1,0:T(8,128)(2,1)} %param.20, bf16[512,4096]{1,0:T(8,128)(2,1)S(1)} %copy-done.10, f32[4096]{0:T(1024)S(1)} %copy-done.18, f32[512]{0:T(512)S(1)} %add_rsqrt_fusion.1), kind=kOutput, calls=%fused_computation.128 | convolution fusion | flops 6451625984 | bytes 18368512 | tf_op jit(solution)/shard_map/rd,jdc->jrc/dot_general | solution.py:108
  75.7 1.2 copy-done.11
  77.1 1.0 pad_maximum_fusion.5
  80.9 54.8 %gather_fusion.1 = f32[16384,32]{1,0:T(8,128)} fusion(f32[32,128]{0,1:T(8,128)S(1)} %copy.81, s32[16384]{0:T(1024)S(1)} %bitcast_clamp_fusion), kind=kCustom, calls=%fused_computation.1.clone | custom fusion | bytes 4259840 | tf_op jit(solution)/shard_map/jit(_take)/gather | solution.py:30
  135.6 6.5 copy.86
  142.1 54.8 %gather_fusion = f32[16384,32]{1,0:T(8,128)} fusion(f32[32,128]{0,1:T(8,128)S(1)} %copy.81, s32[16384]{0:T(1024)S(1)} %bitcast_clamp_fusion.1), kind=kCustom, calls=%fused_computation.clone | custom fusion | bytes 4259840 | tf_op jit(solution)/shard_map/jit(_take)/gather | solution.py:29
  196.9 5.5 copy.82
  202.6 3.4 slice_convert_fusion.2
  206.0 8.8 %fusion.38 = f32[1,3,129,512]{3,0,2,1:T(1,128)S(1)} fusion(bf16[32,3,129,512]{3,2,1,0:T(8,128)(2,1)} %all-gather.9.cloned.1.call-done, s32[32]{0:T(128)S(1)} %copy-done.14, s32[]{:T(128)} %bitcast.22), kind=kOutput, calls=%fused_computation.69 | convolution fusion | flops 12681248 | bytes 13473924 | tf_op jit(solution)/shard_map/s,sjrc->jrc/dot_general | solution.py:127
  214.8 3.7 fusion.40
  218.8 1.2 copy-done.6
  220.4 1.7 fusion.64
  222.5 1.1 copy-done.2
  223.6 1.0 fusion.168
  224.6 1.0 slice_multiply_fusion
  225.7 1.0 copy.84
  226.8 1.3 slice.241
  228.9 2.1 copy.80
  231.0 2.1 slice.239
  233.0 5.0 fusion.71
  238.0 3.4 fusion.89
  241.8 1.0 copy.89
  242.8 1.1 pad_slice_fusion.8
  243.9 1.0 copy.92
  244.9 2.1 slice.254
  247.0 5.2 fusion.69
  253.0 2.1 copy.90
  255.1 2.1 slice.252
  257.2 4.6 fusion.95
  263.1 1.6 fusion.119
  264.7 7.8 %fusion.120 = f32[512,4096]{1,0:T(8,128)} fusion(bf16[512,4096]{1,0:T(8,128)(2,1)} %param.24, bf16[256,512]{1,0:T(8,128)(2,1)S(1)} %get-tuple-element.361, bf16[256,512]{1,0:T(8,128)(2,1)S(1)} %get-tuple-element.360), kind=kOutput, calls=%fused_computation.170 | convolution fusion | flops 2148532224 | bytes 13107200 | tf_op jit(solution)/shard_map/dot_general | solution.py:144
  272.6 81.1 %reduce-scatter.3.cloned.1.call-done = f32[128,4096]{1,0:T(8,128)} async-done(((f32[512,4096]{1,0:T(8,128)}), f32[128,4096]{1,0:T(8,128)}) %reduce-scatter.3.cloned.1.call-update) | async-done | bytes 2097168 | tf_op jit(solution)/shard_map/reduce_scatter | solution.py:143
  353.6 3.1 convert_add_fusion.1
  357.5 82.3 %all-gather.11.cloned.1.call-done = f32[512,4096]{1,0:T(8,128)} async-done(((f32[128,4096]{1,0:T(8,128)}), f32[512,4096]{1,0:T(8,128)}) %all-gather.11.cloned.1.call-update) | async-done | bytes 8388624 | tf_op jit(solution)/shard_map/all_gather | solution.py:150
  439.8 4.2 multiply_reduce_fusion
  444.0 1.6 copy-done.5
  445.6 11.3 %fusion.77 = f32[3,512,512]{1,2,0:T(8,128)} fusion(bf16[3,4096,512]{2,1,0:T(8,128)(2,1)} %param.26, f32[512,4096]{1,0:T(8,128)S(1)} %copy-done.5, f32[4096]{0:T(1024)S(1)} %copy-done.19, f32[512]{0:T(512)S(1)} %add_rsqrt_fusion), kind=kOutput, calls=%fused_computation.126 | convolution fusion | flops 6448742400 | bytes 24135680 | tf_op jit(solution)/shard_map/rd,jdf->jrf/dot_general | solution.py:152
  456.9 1.7 fusion.156
  459.9 2.1 slice.395
  462.4 75.8 %all-gather.13.cloned.1.call-done = bf16[8192,512]{0,1:T(8,128)(2,1)} async-done(((bf16[512,512]{0,1:T(8,128)(2,1)}), bf16[8192,512]{0,1:T(8,128)(2,1)}) %all-gather.13.cloned.1.call-update) | async-done | bytes 8388624 | tf_op jit(solution)/shard_map/all_gather | solution.py:166
  538.2 79.6 %all-gather.15.cloned.1.call-done = bf16[1,8192,512]{1,2,0:T(8,128)(2,1)} async-done(((bf16[1,512,512]{1,2,0:T(8,128)(2,1)}), bf16[1,8192,512]{1,2,0:T(8,128)(2,1)}) %all-gather.15.cloned.1.call-update) | async-done | bytes 8388624 | tf_op jit(solution)/shard_map/all_gather | solution.py:167
  617.9 87.6 %while.20 = (s32[]{:T(128)}, f32[2,256,4]{1,2,0:T(4,128)S(1)}, f32[2,256,4]{1,2,0:T(4,128)S(1)}, f32[2,256,4,128]{1,3,2,0:T(8,128)S(1)}, s32[32]{0:T(128)S(1)}, ...) while((s32[]{:T(128)}, f32[2,256,4]{1,2,0:T(4,128)S(1)}, ...), condition=%wide.region_10.12_spmd.clone, body=%wide.region_4.11_spmd.clone.sunk | while | flops 551627264 | bytes 22718784 | solution.py:217
  618.5 1.3 constant_dynamic-slice_fusion.3
  624.0 1.3 constant_dynamic-slice_fusion.3
  629.4 1.3 constant_dynamic-slice_fusion.3
  634.9 1.3 constant_dynamic-slice_fusion.3
  640.4 1.3 constant_dynamic-slice_fusion.3
  645.8 1.3 constant_dynamic-slice_fusion.3
  651.3 1.3 constant_dynamic-slice_fusion.3
  656.7 1.3 constant_dynamic-slice_fusion.3
  662.2 1.3 constant_dynamic-slice_fusion.3
  667.6 1.3 constant_dynamic-slice_fusion.3
  673.1 1.3 constant_dynamic-slice_fusion.3
  678.6 1.3 constant_dynamic-slice_fusion.3
  684.0 1.3 constant_dynamic-slice_fusion.3
  689.5 1.3 constant_dynamic-slice_fusion.3
  694.9 1.3 constant_dynamic-slice_fusion.3
  700.4 1.3 constant_dynamic-slice_fusion.3
  705.9 6.5 convolution_convert_fusion
  712.4 47.5 %reduce-scatter.5.cloned.1.call-done = bf16[128,4096]{1,0:T(8,128)(2,1)} async-done(((bf16[512,4096]{1,0:T(8,128)(2,1)}), bf16[128,4096]{1,0:T(8,128)(2,1)}) %reduce-scatter.5.cloned.1.call-update) | async-done | bytes 1048592 | tf_op jit(solution)/shard_map/reduce_scatter | solution.py:225
  759.9 2.7 convert_add_fusion
  (347 shorter events, 74.3 us)
Async XLA Ops:
  6.5 55.8 %all-gather.7.cloned.1.call-start = ((), (), s32[]{:S(2)}) async-start(), calls=%async_computation.2 | async-start | bytes 5242880 | tf_op jit(solution)/shard_map/all_gather | solution.py:106
  10.5 55.1 %copy-start.18 = (f32[4096]{0:T(1024)S(1)}, f32[4096]{0:T(1024)}, u32[]{:S(2)}) copy-start(f32[4096]{0:T(1024)} %param.19) | copy-start | bytes 49156
  10.5 195.5 %all-gather.9.cloned.1.call-start = ((), (), s32[]{:S(2)}) async-start(), calls=%async_computation.3 | async-start | bytes 14204928 | tf_op jit(solution)/shard_map/all_gather | solution.py:122
  62.3 3.4 copy-start.10
  75.7 1.2 copy-start.11
  76.8 1.9 copy-start.14
  76.8 3.8 copy-start.16
  76.9 3.9 copy-start.15
  78.1 275.5 %reduce-scatter.3.cloned.1.call-start = ((), (), s32[]{:S(2)}) async-start(), calls=%async_computation.4 | async-start | bytes 10485760 | tf_op jit(solution)/shard_map/reduce_scatter | solution.py:143
  206.0 8.8 %copy-start = (bf16[32,3,129,512]{3,2,1,0:T(8,128)(2,1)S(1)}, bf16[32,3,129,512]{3,2,1,0:T(8,128)(2,1)}, u32[]{:S(2)}) copy-start(bf16[32,3,129,512]{3,2,1,0:T(8,128)(2,1)} %all-gather.9.cloned.1.call-done) | copy-start | bytes 38043652
  218.6 1.4 copy-start.6
  218.6 1.9 copy-start.7
  222.2 1.4 copy-start.2
  222.2 2.4 copy-start.3
  233.0 5.0 copy-start.13
  247.0 5.2 copy-start.8
  261.8 1.1 copy-start.9
  261.8 1.3 copy-start.12
  261.8 1.3 copy-start.17
  272.5 81.2 %copy-start.4 = (bf16[128,4096]{1,0:T(8,128)(2,1)S(1)}, bf16[128,4096]{1,0:T(8,128)(2,1)}, u32[]{:S(2)}) copy-start(bf16[128,4096]{1,0:T(8,128)(2,1)} %convolution_convert_fusion.1) | copy-start | bytes 3145732
  272.5 167.3 %all-gather.11.cloned.1.call-start = ((), (), s32[]{:S(2)}) async-start(), calls=%async_computation.5 | async-start | bytes 10485760 | tf_op jit(solution)/shard_map/all_gather | solution.py:150
  356.8 181.4 %all-gather.13.cloned.1.call-start = ((), (), s32[]{:S(2)}) async-start(), calls=%async_computation.6 | async-start | bytes 8912896 | tf_op jit(solution)/shard_map/all_gather | solution.py:166
  356.9 87.0 %copy-start.19 = (f32[4096]{0:T(1024)S(1)}, f32[4096]{0:T(1024)}, u32[]{:S(2)}) copy-start(f32[4096]{0:T(1024)} %param.25) | copy-start | bytes 49156
  439.8 5.8 copy-start.5
  459.8 158.0 %all-gather.15.cloned.1.call-start = ((), (), s32[]{:S(2)}) async-start(), calls=%async_computation.8 | async-start | bytes 8912896 | tf_op jit(solution)/shard_map/all_gather | solution.py:167
  462.0 297.9 %reduce-scatter.5.cloned.1.call-start = ((), (), s32[]{:S(2)}) async-start(), calls=%async_computation.7 | async-start | bytes 5242880 | tf_op jit(solution)/shard_map/reduce_scatter | solution.py:225
  712.4 47.6 %copy-start.1 = (f32[128,4096]{1,0:T(8,128)S(1)}, f32[128,4096]{1,0:T(8,128)}, u32[]{:S(2)}) copy-start(f32[128,4096]{1,0:T(8,128)} %convert_add_fusion.1) | copy-start | bytes 6291460
Sparse Core Ops, SparseCore 0:
  10.6 51.6 all-gather.6
  78.2 93.9 all-gather.8
  272.6 80.9 reduce-scatter.2
  356.9 82.8 all-gather.10
  459.9 78.1 all-gather.12
  540.1 77.6 all-gather.14
  712.5 47.3 reduce-scatter.4
where the time goes:
time: 775 us; the launch traced here: 770 us
  waiting for transfers between devices  418 us (54%)
  local copies, waits for them, and re-layouts  172 us (22%)
  matrix products  111 us (14%)
  other arithmetic  49.8 us (6%)
  between operations  15.3 us (2%)
    all_gather x1, waiting for transfers between devices, body(): stream_all = lax.all_gather(stream_own, 'tensor', axis=0, tiled=True)  82.3 us
    reduce_scatter x1, waiting for transfers between devices, body(): lax.psum_scatter(jnp.dot(hyena_mix, hyena_out, preferred_element_type=jnp...  81.1 us
    all_gather x1, waiting for transfers between devices, body(): value_piece = lax.all_gather(values_flat, 'context', axis=0, tiled=True)  79.6 us
    all_gather x1, waiting for transfers between devices, body(): key_piece = lax.all_gather(keys_flat, 'context', axis=0, tiled=True)  75.8 us
    gather x2, local copies, waits for them, and re-layouts, toeplitz(): jnp.take(long_filter, jnp.clip(tap_lag + filter_len, 0, filter_len - 1),...  61.2 us
    gather x2, local copies, waits for them, and re-layouts, toeplitz(): jnp.take(long_filter, jnp.clip(tap_lag, 0, filter_len - 1), axis=1)  60.3 us
    all_gather x1, waiting for transfers between devices, body(): embedded_all = lax.all_gather(embedded, 'tensor', axis=0, tiled=True)  51.8 us
    reduce_scatter x1, waiting for transfers between devices, body(): lax.psum_scatter(jnp.dot(attended, attn_out, preferred_element_type=jnp.f...  47.5 us
  transfers between devices with their start and end apart: 7, of which 6 were waited for; matrix products, arithmetic and copies ran while one was open for 17% of the time, Pallas kernels for 0%

commit v1 on v0

v1 whole, which is shorter than its diff:
```python
import functools
import math

import jax
import jax.numpy as jnp
from jax import lax
from jax.experimental import pallas as pl
from jax.experimental.pallas import tpu as pltpu
from jax.sharding import PartitionSpec as P

HD = 128
EPS = 1e-06
THETA = 1000000.0
NEG_FILL = -1e30
CODES = (65, 67, 71, 84)
MESH_ID = pl.DeviceIdType.MESH
F32 = jnp.float32
BF16 = jnp.bfloat16
ANY = pl.BlockSpec(memory_space=pl.ANY)


def coords():
    dp = lax.axis_index("dp")
    ctx = lax.axis_index("context")
    t = lax.axis_index("tensor")
    return dp, ctx // 4, ctx % 4, t


def pick(dp, first, second):
    return first + dp * (second - first)


def remote(src, dst, send, recv, where):
    return pltpu.make_async_remote_copy(
        src_ref=src, dst_ref=dst, send_sem=send, recv_sem=recv, device_id=where, device_id_type=MESH_ID
    )


ZKINDS = ((3, 0), (3, 1), (1, 0), (1, 1), (2, 0), (2, 1))


class WeightGather:
    def __init__(self, w_in, w_out, send, recv, local_sem):
        self.w_in, self.w_out, self.send, self.recv, self.local_sem = w_in, w_out, send, recv, local_sem
        dp, y, x, t = coords()
        self.dp, self.t = dp, t
        u, w = pick(dp, x, y), pick(dp, y, x)
        self.q = (u + 2 * w) % 4
        self.sib_q = (w + 2 * u) % 4
        self.shard = w_in.shape[0]
        self.piece = self.shard // 16
        xp, xm, yp, ym = (x + 1) % 4, (x + 3) % 4, (y + 1) % 4, (y + 3) % 4
        self.up = {"context": pick(dp, y * 4 + xp, yp * 4 + x)}
        self.um = {"context": pick(dp, y * 4 + xm, ym * 4 + x)}
        self.wp = {"context": pick(dp, yp * 4 + x, y * 4 + xp)}
        self.wm = {"context": pick(dp, ym * 4 + x, y * 4 + xm)}
        self.zp = {"tensor": (t + 1) % 4}
        self.zm = {"tensor": (t + 3) % 4}
        self.sib = {"dp": 1 - dp}
        self.pending = []

    def unit(self, z, dp, q, h):
        start = z * self.shard + dp * (self.shard // 2) + q * (2 * self.piece) + h * self.piece
        return self.w_out.at[pl.ds(pl.multiple_of(start, self.piece), self.piece), :]

    def own(self, h):
        start = self.dp * (self.shard // 2) + self.q * (2 * self.piece) + h * self.piece
        return self.w_in.at[pl.ds(pl.multiple_of(start, self.piece), self.piece), :]

    def go(self, src, dst, recv_at, where):
        at = len(self.pending)
        copy = remote(src, dst, self.send.at[at], self.recv.at[recv_at], where)
        copy.start()
        self.pending.append(copy)

    def arrived(self, dst, recv_at):
        remote(dst, dst, self.send.at[0], self.recv.at[recv_at], self.sib).wait_recv()

    def start(self):
        row = pl.multiple_of(self.t * self.shard, self.shard)
        self.local = pltpu.make_async_copy(self.w_in, self.w_out.at[pl.ds(row, self.shard), :], self.local_sem)
        self.local.start()
        for h in (0, 1):
            dst = self.unit(self.t, self.dp, self.q, h)
            first, second = ((self.zp, 0 + h), (self.zm, 2 + h))
            if h == 0:
                self.go(self.own(h), dst, first[1], first[0])
                self.go(self.own(1), self.unit(self.t, self.dp, self.q, 1), 3, self.zm)
            else:
                self.go(self.own(1), dst, 1, self.zp)
                self.go(self.own(0), self.unit(self.t, self.dp, self.q, 0), 2, self.zm)

    def z_step(self, kind):
        zoff, h = ZKINDS[kind]
        ref = self.unit((self.t + zoff) % 4, self.dp, self.q, h)
        self.arrived(ref, kind)
        if kind == 0:
            self.go(ref, ref, 4, self.zp)
        if kind == 3:
            self.go(ref, ref, 5, self.zm)
        self.go(ref, ref, 6 + kind, self.up)
        self.go(ref, ref, 12 + kind, self.um)
        self.go(ref, ref, 18 + kind, self.wp if h == 0 else self.wm)
        self.go(ref, ref, 24 + kind, self.sib)

    def plane_ref(self, side, kind, dp, q):
        zoff, h = ZKINDS[kind]
        qoff = (3, 1, 2)[side]
        return self.unit((self.t + zoff) % 4, dp, (q + qoff) % 4, h)

    def plane_step(self, side, kind):
        at = 6 + 6 * side + kind
        ref = self.plane_ref(side, kind, self.dp, self.q)
        self.arrived(ref, at)
        self.go(ref, ref, 24 + at, self.sib)

    def finish(self):
        for kind in range(6):
            zoff, h = ZKINDS[kind]
            self.arrived(self.unit((self.t + zoff) % 4, 1 - self.dp, self.sib_q, h), 24 + kind)
            for side in range(3):
                self.arrived(self.plane_ref(side, kind, 1 - self.dp, self.sib_q), 30 + 6 * side + kind)
        for copy in self.pending:
            copy.wait_send()
        self.local.wait()


KIND_ORDER = (0, 3, 1, 2, 4, 5)
N_SENDS = 6 + 18 + 24


def gather_kernel(ids_ref, pack_ref, wh_ref, wa_ref, ids_out, pack_out, wh_out, wa_out,
                  sh, rh, sa, ra, s_ids, r_ids, s_pack, r_pack, loc):
    dp, y, x, t = coords()
    ctx = y * 4 + x
    barrier = pltpu.get_barrier_semaphore()
    partners = (
        [{"tensor": (t + d) % 4} for d in (1, 2, 3)]
        + [{"context": y * 4 + (x + d) % 4} for d in (1, 2, 3)]
        + [{"context": ((y + d) % 4) * 4 + x} for d in (1, 2, 3)]
        + [{"dp": 1 - dp}]
    )
    for where in partners:
        pl.semaphore_signal(barrier, inc=1, device_id=where, device_id_type=MESH_ID)
    pl.semaphore_wait(barrier, len(partners))

    small = []
    mine = ctx * 4 + t
    keep_ids = pltpu.make_async_copy(ids_ref, ids_out.at[pl.ds(mine, 1)], loc.at[2])
    keep_ids.start()
    keep_pack = pltpu.make_async_copy(pack_ref, pack_out.at[t], loc.at[3])
    keep_pack.start()
    for d in (1, 2, 3):
        c = remote(ids_ref, ids_out.at[pl.ds(mine, 1)], s_ids.at[d - 1], r_ids.at[d - 1], partners[d - 1])
        c.start()
        small.append(c)
        c = remote(pack_ref, pack_out.at[t], s_pack.at[d - 1], r_pack.at[d - 1], partners[d - 1])
        c.start()
        small.append(c)
    gh = WeightGather(wh_ref, wh_out, sh, rh, loc.at[0])
    ga = WeightGather(wa_ref, wa_out, sa, ra, loc.at[1])
    gh.start()
    keep_ids.wait()
    for d in (1, 2, 3):
        ref = ids_out.at[pl.ds(ctx * 4 + (t + 4 - d) % 4, 1)]
        remote(ref, ref, s_ids.at[0], r_ids.at[d - 1], partners[0]).wait_recv()
    row = ids_out.at[pl.ds(ctx * 4, 4)]
    for d in (1, 2, 3):
        c = remote(row, row, s_ids.at[2 + d], r_ids.at[2 + d], partners[2 + d])
        c.start()
        small.append(c)
    for d in (1, 2, 3):
        ref = ids_out.at[pl.ds((y * 4 + (x + 4 - d) % 4) * 4, 4)]
        remote(ref, ref, s_ids.at[0], r_ids.at[2 + d], partners[0]).wait_recv()
    row = ids_out.at[pl.ds(y * 16, 16)]
    for d in (1, 2, 3):
        c = remote(row, row, s_ids.at[5 + d], r_ids.at[5 + d], partners[5 + d])
        c.start()
        small.append(c)
    for k in KIND_ORDER:
        gh.z_step(k)
    ga.start()
    for k in KIND_ORDER:
        for side in range(3):
            gh.plane_step(side, k)
    for k in KIND_ORDER:
        ga.z_step(k)
    gh.finish()
    for k in KIND_ORDER:
        for side in range(3):
            ga.plane_step(side, k)
    ga.finish()
    for d in (1, 2, 3):
        ref = ids_out.at[pl.ds(((y + 4 - d) % 4) * 16, 16)]
        remote(ref, ref, s_ids.at[0], r_ids.at[5 + d], partners[0]).wait_recv()
        ref = pack_out.at[(t + 4 - d) % 4]
        remote(ref, ref, s_ids.at[0], r_pack.at[d - 1], partners[0]).wait_recv()
    for c in small:
        c.wait_send()
    keep_pack.wait()


def gather_all(ids, pack, wh, wa):
    dma = pltpu.SemaphoreType.DMA
    return pl.pallas_call(
        gather_kernel,
        out_shape=(
            jax.ShapeDtypeStruct((64, 1, 128), jnp.int32),
            jax.ShapeDtypeStruct((4,) + pack.shape, F32),
            jax.ShapeDtypeStruct((2048, 4096), BF16),
            jax.ShapeDtypeStruct((2048, 4096), BF16),
        ),
        in_specs=[ANY] * 4,
        out_specs=(ANY,) * 4,
        scratch_shapes=[
            dma((N_SENDS,)), dma((48,)), dma((N_SENDS,)), dma((48,)),
            dma((9,)), dma((9,)), dma((3,)), dma((3,)), dma((4,)),
        ],
        compiler_params=pltpu.CompilerParams(collective_id=0, has_side_effects=True),
        name="gather_all",
    )(ids, pack, wh, wa)


def mix_kernel(onehot_ref, tab_ref, taps_ref, skip_ref, out_ref):
    table = jnp.concatenate([tab_ref[0], tab_ref[1], tab_ref[2]], axis=1)
    high = table.astype(BF16)
    low = (table - high.astype(F32)).astype(BF16)
    both = jnp.concatenate([high, low], axis=0)
    filtered = jnp.dot(onehot_ref[...], both, preferred_element_type=F32)
    gated = filtered[:, 128:256] * filtered[:, 256:384]
    g16 = gated.astype(BF16)
    window = jnp.concatenate(
        [g16[b * 384 + s * 128 : b * 384 + s * 128 + 256] for b in range(2) for s in range(2)], axis=1
    )
    lane_group = (lax.broadcasted_iota(jnp.int32, window.shape, 1) % 128) // 16
    total = jnp.zeros((128, 512), F32)
    for g in range(8):
        base = jnp.broadcast_to(taps_ref[g : g + 1, :], (128, 256))
        toep = pltpu.roll(base, 0, 1, stride=1, stride_axis=0).astype(BF16)
        masked = jnp.where(lane_group == g, window, jnp.zeros_like(window))
        total = total + jnp.dot(toep, masked, preferred_element_type=F32)
    for b in range(2):
        for s in range(2):
            at = b * 384 + 128 + s * 128
            part = total[:, (2 * b + s) * 128 : (2 * b + s + 1) * 128]
            mixed = filtered[at : at + 128, 0:128] * (part + skip_ref[...] * gated[at : at + 128])
            out_ref[b * 256 + s * 128 : b * 256 + (s + 1) * 128, :] = mixed.astype(BF16)


def hyena_mix(onehot, tab, taps, skip):
    return pl.pallas_call(
        mix_kernel,
        out_shape=jax.ShapeDtypeStruct((512, 2048), BF16),
        grid=(16,),
        in_specs=[
            pl.BlockSpec((768, 32), lambda i: (0, 0)),
            pl.BlockSpec((3, 16, 128), lambda i: (0, 0, i)),
            pl.BlockSpec((8, 256), lambda i: (i, 0)),
            pl.BlockSpec((1, 128), lambda i: (0, i)),
        ],
        out_specs=pl.BlockSpec((512, 128), lambda i: (0, i)),
        compiler_params=pltpu.CompilerParams(vmem_limit_bytes=40 * 2**20),
        name="hyena_mix",
    )(onehot, tab, taps, skip)


def proj_kernel(t_ref, mix_ref, wh_ref, code_ref, emb_ref, gain_ref, wq_ref, cos_ref, sin_ref,
                own_ref, qkv_ref, attn_in, chunk, squares):
    i = pl.program_id(0)

    @pl.when(i < 8)
    def _():
        vals = jnp.dot(mix_ref[...], wh_ref[...], preferred_element_type=F32)
        vals = vals + jnp.dot(code_ref[...], emb_ref[...], preferred_element_type=F32)
        chunk[...] = vals
        part = jnp.sum(vals * vals, axis=1, keepdims=True)

        @pl.when(i == 0)
        def _():
            squares[...] = jnp.zeros_like(squares)

        squares[...] += jnp.broadcast_to(part, squares.shape)
        attn_in[:, pl.ds(pl.multiple_of(i * 512, 512), 512)] = (vals * gain_ref[...]).astype(BF16)
        own_ref[...] = chunk[pl.ds(pl.multiple_of(t_ref[0] * 128, 128), 128), :]

    @pl.when(i >= 8)
    def _():
        k = i - 8
        j = k // 2
        factor = lax.rsqrt(squares[...] / 4096.0 + EPS)
        factor = factor * jnp.where(j == 0, HD**-0.5 * math.log2(math.e), 1.0).astype(F32)
        rotated = j < 2
        cos = jnp.where(rotated, cos_ref[...], 1.0) * factor
        sin = jnp.where(rotated, sin_ref[...], 0.0) * factor
        vals = jnp.dot(attn_in[...], wq_ref[0], preferred_element_type=F32)
        for hh in range(2):
            head = vals[:, hh * 128 : (hh + 1) * 128]
            turned = head * cos + pltpu.roll(head, 64, 1) * sin
            qkv_ref[2 * (k % 2) + hh, j] = turned.astype(BF16).reshape(2, 4, 64, 128)


def stream_qkv(t_arr, mix, wh, code_hot, emb4, gain, wq, cos, sin):
    def whi(i, t):
        return (0, jnp.minimum(i, 7))

    def wqi(i, t):
        k = jnp.maximum(i - 8, 0)
        return (k // 2, 0, k % 2)

    def whole(*shape):
        return pl.BlockSpec(shape, lambda i, t: (0,) * len(shape))

    return pl.pallas_call(
        proj_kernel,
        out_shape=(
            jax.ShapeDtypeStruct((128, 4096), F32),
            jax.ShapeDtypeStruct((4, 3, 2, 4, 64, 128), BF16),
        ),
        grid_spec=pltpu.PrefetchScalarGridSpec(
            num_scalar_prefetch=1,
            grid=(14,),
            in_specs=[
                whole(512, 2048),
                pl.BlockSpec((2048, 512), whi),
                whole(512, 16),
                pl.BlockSpec((16, 512), whi),
                pl.BlockSpec((1, 512), whi),
                pl.BlockSpec((1, 4096, 256), wqi),
                whole(512, 128),
                whole(512, 128),
            ],
            out_specs=(
                pl.BlockSpec((128, 512), whi),
                whole(4, 3, 2, 4, 64, 128),
            ),
            scratch_shapes=[
                pltpu.VMEM((512, 4096), BF16),
                pltpu.VMEM((512, 512), F32),
                pltpu.VMEM((512, 128), F32),
            ],
        ),
        compiler_params=pltpu.CompilerParams(vmem_limit_bytes=48 * 2**20),
        name="stream_qkv",
    )(t_arr, mix, wh, code_hot, emb4, gain, wq, cos, sin)


def ab_of(dp, y, x):
    return pick(dp, y, x), pick(dp, x, y)


def ctx_of(dp, a, b):
    return pick(dp, a * 4 + b, b * 4 + a)


def exchange_kernel(qkv_ref, q_out, kv_out, sq, rq, s1, r1, s2, r2, s3, r3, loc):
    dp, y, x, t = coords()
    ctx = y * 4 + x
    a, b = ab_of(dp, y, x)
    barrier = pltpu.get_barrier_semaphore()
    others = [{"context": (ctx + d) % 16} for d in range(1, 16)]
    for where in others:
        pl.semaphore_signal(barrier, inc=1, device_id=where, device_id_type=MESH_ID)
    pl.semaphore_wait(barrier, 15)
    sent = []
    keep_kv = pltpu.make_async_copy(qkv_ref.at[a, pl.ds(1, 2)], kv_out.at[ctx], loc.at[0])
    keep_kv.start()
    bp = {"context": ctx_of(dp, a, (b + 1) % 4)}
    bm = {"context": ctx_of(dp, a, (b + 3) % 4)}

    def spread(src, k, src_ctx):
        for side, where in ((0, bp), (1, bm)):
            c = remote(src, kv_out.at[src_ctx], s2.at[side * 4 + k], r2.at[side * 4 + k], where)
            c.start()
            sent.append(c)

    for d in (1, 3, 2):
        h = (a + d) % 4
        c = remote(qkv_ref.at[h, pl.ds(1, 2)], kv_out.at[ctx], s1.at[d - 1], r1.at[d - 1], {"context": ctx_of(dp, h, b)})
        c.start()
        sent.append(c)
    spread(qkv_ref.at[a, pl.ds(1, 2)], 0, ctx)
    for d in range(1, 16):
        to = (ctx + d) % 16
        h, s = ab_of(dp, to // 4, to % 4)
        c = remote(qkv_ref.at[h, 0, :, s], q_out.at[ctx], sq.at[d - 1], rq.at[d - 1], others[d - 1])
        c.start()
        sent.append(c)
    keep_q = pltpu.make_async_copy(qkv_ref.at[a, 0, :, b], q_out.at[ctx], loc.at[1])
    keep_q.start()
    for d in (1, 3, 2):
        from_ctx = ctx_of(dp, (a + 4 - d) % 4, b)
        ref = kv_out.at[from_ctx]
        remote(ref, ref, s1.at[0], r1.at[d - 1], bp).wait_recv()
        spread(ref, d, from_ctx)
    for k in (0, 1, 3, 2):
        ua = (a + 4 - k) % 4
        ref = kv_out.at[ctx_of(dp, ua, (b + 3) % 4)]
        remote(ref, ref, s1.at[0], r2.at[k], bp).wait_recv()
        c = remote(ref.at[0], ref.at[0], s3.at[k], r3.at[k], bp)
        c.start()
        sent.append(c)
        ref = kv_out.at[ctx_of(dp, ua, (b + 1) % 4)]
        remote(ref, ref, s1.at[0], r2.at[4 + k], bp).wait_recv()
        c = remote(ref.at[1], ref.at[1], s3.at[4 + k], r3.at[4 + k], bm)
        c.start()
        sent.append(c)
    for k in (0, 1, 3, 2):
        ref = kv_out.at[ctx_of(dp, (a + 4 - k) % 4, (b + 2) % 4)]
        for part in (0, 1):
            remote(ref.at[part], ref.at[part], s1.at[0], r3.at[4 * part + k], bp).wait_recv()
    for d in range(1, 16):
        ref = q_out.at[(ctx + 16 - d) % 16]
        remote(ref, ref, s1.at[0], rq.at[d - 1], bp).wait_recv()
    for c in sent:
        c.wait_send()
    keep_q.wait()
    keep_kv.wait()


def exchange(qkv):
    dma = pltpu.SemaphoreType.DMA
    return pl.pallas_call(
        exchange_kernel,
        out_shape=(
            jax.ShapeDtypeStruct((16, 2, 64, 128), BF16),
            jax.ShapeDtypeStruct((16, 2, 2, 4, 64, 128), BF16),
        ),
        in_specs=[ANY],
        out_specs=(ANY,) * 2,
        scratch_shapes=[dma((15,)), dma((15,)), dma((3,)), dma((3,)), dma((8,)), dma((8,)), dma((8,)), dma((8,)), dma((2,))],
        compiler_params=pltpu.CompilerParams(collective_id=1, has_side_effects=True),
        name="exchange",
    )(qkv)


KEYS = 1024


def attend_kernel(slot_ref, q_hbm, kv_hbm, o_hbm, q_s, k_s, v_s, o_s, sem, osem):
    b = slot_ref[32]

    def load(p, _):
        slot = slot_ref[p]
        c, i = slot // 2, slot % 2
        pltpu.make_async_copy(q_hbm.at[c, i], q_s.at[pl.ds(pl.multiple_of(p * 64, 64), 64)], sem.at[0, p]).start()
        rows = pl.ds(pl.multiple_of(p * 256, 256), 256)
        pltpu.make_async_copy(kv_hbm.at[c, 0, i], k_s.at[rows], sem.at[1, p]).start()
        pltpu.make_async_copy(kv_hbm.at[c, 1, i], v_s.at[rows], sem.at[2, p]).start()
        return 0

    lax.fori_loop(0, 32, load, 0)

    for j in range(8):
        for p in range(4 * j, 4 * j + 4):
            pltpu.make_async_copy(q_hbm.at[0, 0], q_s.at[pl.ds(p * 64, 64)], sem.at[0, p]).wait()
            pltpu.make_async_copy(kv_hbm.at[0, 0, 0], k_s.at[pl.ds(p * 256, 256)], sem.at[1, p]).wait()
            pltpu.make_async_copy(kv_hbm.at[0, 1, 0], v_s.at[pl.ds(p * 256, 256)], sem.at[2, p]).wait()
        q = q_s[pl.ds(j * 256, 256), :]

        def step(start, carry, masked):
            top, tot, acc = carry
            keys = k_s[pl.ds(start, KEYS), :]
            scores = lax.dot_general(q, keys, (((1,), (1,)), ((), ())), preferred_element_type=F32)
            if masked:
                r = lax.broadcasted_iota(jnp.int32, scores.shape, 0)
                col = lax.broadcasted_iota(jnp.int32, scores.shape, 1)
                qpos = (r // 64) * 256 + b * 64 + r % 64
                scores = jnp.where(col <= qpos, scores, NEG_FILL)
            new = jnp.maximum(top, jnp.max(scores, axis=1, keepdims=True))
            w = jnp.exp2(scores - new)
            shrink = jnp.exp2(top - new)
            tot = tot * shrink + jnp.sum(w, axis=1, keepdims=True)
            acc = acc * shrink + jnp.dot(w.astype(BF16), v_s[pl.ds(start, KEYS), :], preferred_element_type=F32)
            return new, tot, acc

        first = (jnp.full((256, 1), NEG_FILL, F32), jnp.zeros((256, 1), F32), jnp.zeros((256, 128), F32))
        carry = step(j * KEYS, first, True)
        if j:
            carry = lax.fori_loop(0, j, lambda kc, c: step(pl.multiple_of(kc * KEYS, KEYS), c, False), carry)
        top, tot, acc = carry
        o_s[pl.ds(j * 256, 256), :] = (acc / tot).astype(BF16)
        for p in range(4 * j, 4 * j + 4):
            pltpu.make_async_copy(o_s.at[pl.ds(p * 64, 64)], o_hbm.at[slot_ref[p]], osem.at[p]).start()
    for p in range(32):
        pltpu.make_async_copy(o_s.at[pl.ds(p * 64, 64)], o_hbm.at[0], osem.at[p]).wait()


def attend(slots, q_all, kv_all):
    dma = pltpu.SemaphoreType.DMA
    return pl.pallas_call(
        attend_kernel,
        out_shape=jax.ShapeDtypeStruct((32, 64, 128), BF16),
        in_specs=[pl.BlockSpec(memory_space=pltpu.SMEM), ANY, ANY],
        out_specs=ANY,
        scratch_shapes=[
            pltpu.VMEM((2048, 128), BF16),
            pltpu.VMEM((8192, 128), BF16),
            pltpu.VMEM((8192, 128), BF16),
            pltpu.VMEM((2048, 128), BF16),
            dma((3, 32)),
            dma((32,)),
        ],
        compiler_params=pltpu.CompilerParams(vmem_limit_bytes=48 * 2**20),
        name="attend",
    )(slots, q_all, kv_all)


def return_kernel(o_ref, att_out, send, recv, loc):
    dp, y, x, t = coords()
    ctx = y * 4 + x
    a, b = ab_of(dp, y, x)
    barrier = pltpu.get_barrier_semaphore()

    def source(n):
        st, sa, r = n // 8, (n // 2) % 4, n % 2
        return st, ctx_of(dp, sa, 2 * (t % 2) + r)

    def dest(n):
        return 2 * (n % 2) + b // 2, n // 2

    def hello(n, _):
        st, sc = source(n)

        @pl.when(jnp.logical_or(st != t, sc != ctx))
        def _():
            pl.semaphore_signal(barrier, inc=1, device_id={"context": sc, "tensor": st}, device_id_type=MESH_ID)

        return 0

    lax.fori_loop(0, 32, hello, 0)
    has_self = (b // 2 == t % 2).astype(jnp.int32)
    pl.semaphore_wait(barrier, 32 - has_self)
    mine = (t * 4 + a) * 2 + b % 2

    def out_copy(n):
        dt, dc = dest(n)
        return remote(o_ref.at[n], att_out.at[mine], send.at[n], recv.at[mine], {"context": dc, "tensor": dt}), dt, dc

    def start(k, _):
        n = (k + 2 * ctx) % 32
        copy, dt, dc = out_copy(n)
        self_copy = jnp.logical_and(dt == t, dc == ctx)

        @pl.when(jnp.logical_not(self_copy))
        def _():
            copy.start()

        @pl.when(self_copy)
        def _():
            pltpu.make_async_copy(o_ref.at[n], att_out.at[mine], loc).start()

        return 0

    lax.fori_loop(0, 32, start, 0)

    def finish(n, _):
        st, sc = source(n)

        @pl.when(jnp.logical_or(st != t, sc != ctx))
        def _():
            ref = att_out.at[n]
            remote(ref, ref, send.at[0], recv.at[n], {"dp": 1 - dp}).wait_recv()

        copy, dt, dc = out_copy(n)
        self_copy = jnp.logical_and(dt == t, dc == ctx)

        @pl.when(jnp.logical_not(self_copy))
        def _():
            copy.wait_send()

        @pl.when(self_copy)
        def _():
            pltpu.make_async_copy(o_ref.at[n], att_out.at[mine], loc).wait()

        return 0

    lax.fori_loop(0, 32, finish, 0)


def give_back(o):
    dma = pltpu.SemaphoreType.DMA
    return pl.pallas_call(
        return_kernel,
        out_shape=jax.ShapeDtypeStruct((32, 64, 128), BF16),
        in_specs=[ANY],
        out_specs=ANY,
        scratch_shapes=[dma((32,)), dma((32,)), dma],
        compiler_params=pltpu.CompilerParams(collective_id=2, has_side_effects=True),
        name="give_back",
    )(o)


def body(ids, block_order, embed, mix_gain, in_proj, short_filter, long_filter, conv_skip,
         hyena_out, attn_gain, qkv_proj, attn_out):
    dp, y, x, t = coords()
    ctx = y * 4 + x
    codes = jnp.array(CODES, jnp.int32)
    emb4 = jnp.concatenate([embed[c : c + 1] for c in CODES] + [jnp.zeros((12, embed.shape[1]), BF16)], axis=0)
    wide = emb4.astype(F32)
    normed = (wide * lax.rsqrt(jnp.mean(wide * wide, axis=-1, keepdims=True) + EPS) * mix_gain).astype(BF16)
    projected = jnp.einsum("rd,jdc->jrc", normed, in_proj, preferred_element_type=F32).astype(BF16)[:, :4]
    table = short_filter[:, :, None, :] * projected.astype(F32)[:, None]
    pack = jnp.concatenate(
        [table.reshape(-1), long_filter.reshape(-1), conv_skip.reshape(-1)]
    ).reshape(-1, 128)
    ids_all, packs, wh, wa = gather_all(ids.reshape(1, 1, 128), pack, hyena_out, attn_out)

    packs = packs.reshape(4, -1)
    n_tab = 36 * 512
    tab = packs[:, :n_tab].reshape(4, 3, 12, 512).transpose(1, 2, 0, 3).reshape(3, 12, 2048)
    tab = jnp.concatenate([tab, jnp.zeros((3, 4, 2048), F32)], axis=1)
    lf = packs[:, n_tab : n_tab + 4096].reshape(128, 128)
    skip = packs[:, n_tab + 4096 :].reshape(1, 2048)
    taps = jnp.concatenate([jnp.zeros((128, 1), F32), lf[:, ::-1], jnp.zeros((128, 127), F32)], axis=1)

    ids_blocks = ids_all.reshape(32, 256)
    slot_ids = jnp.arange(32, dtype=jnp.int32)
    pair = 2 * ctx + jnp.arange(2, dtype=jnp.int32)
    owned = jnp.sum(jnp.where(slot_ids[None] == pair[:, None], block_order[None], 0), axis=1)
    own_ids = lax.dynamic_slice_in_dim(ids_blocks, 2 * ctx, 2, 0)
    hit = block_order[None, :] == owned[:, None] - 1
    prev_ids = jnp.sum(jnp.where(hit[:, :, None], ids_blocks[None, :, 126:], 0), axis=1)
    ext = jnp.concatenate([prev_ids, own_ids], axis=1)
    hots = [
        (ext[:, 2 - tap : 2 - tap + 384, None] == codes).astype(BF16) for tap in range(3)
    ]
    hot16 = jnp.concatenate(hots + [jnp.zeros((2, 384, 4), BF16)], axis=-1).reshape(768, 16)
    hot32 = jnp.concatenate([hot16, hot16], axis=1)
    code_hot = jnp.concatenate(
        [(own_ids.reshape(512, 1) == codes).astype(BF16), jnp.zeros((512, 12), BF16)], axis=1
    )
    mix = hyena_mix(hot32, tab, taps, skip)

    local_pos = (owned[:, None] * 256 + jnp.arange(256, dtype=jnp.int32)[None]).reshape(512)
    inverse_freq = THETA ** (-(2.0 * jnp.arange(64, dtype=F32)) / HD)
    angles = local_pos.astype(F32)[:, None] * inverse_freq[None, :]
    cos, sin = jnp.cos(angles), jnp.sin(angles)
    cos = jnp.concatenate([cos, cos], axis=1)
    sin = jnp.concatenate([-sin, sin], axis=1)
    stream_own, qkv = stream_qkv(
        t.astype(jnp.int32).reshape(1), mix, wh, code_hot, emb4, attn_gain.reshape(1, -1), qkv_proj, cos, sin
    )
    q_all, kv_all = exchange(qkv)
    slot_of = jnp.sum(jnp.where(block_order[None, :] == slot_ids[:, None], slot_ids[None, :], 0), axis=1)
    _, b = ab_of(dp, y, x)
    slots = jnp.concatenate([slot_of, b.astype(jnp.int32).reshape(1)])
    att = attend(slots, q_all, kv_all.reshape(16, 2, 2, 256, 128))
    att = give_back(att)
    att = att.reshape(16, 128, 128).transpose(1, 0, 2).reshape(128, 2048)
    return stream_own + jnp.dot(att, wa, preferred_element_type=F32)


def solution(mesh):
    placed = (
        P(("dp", "context", "tensor")),
        P("dp"),
        P(),
        P(),
        P(None, None, "tensor"),
        P(None, None, "tensor"),
        P("tensor", None),
        P("tensor"),
        P("tensor", None),
        P(),
        P(None, None, "tensor"),
        P("tensor", None),
    )
    return jax.shard_map(
        body,
        mesh=mesh,
        in_specs=placed,
        out_specs=P(("dp", "context", "tensor"), None),
        check_vma=False,
    )
```

time: 775 us -> 426 us (0.55)
  waiting for transfers between devices: 418 us -> 0 us
  Pallas kernels: 0 us -> 391 us
  local copies, waits for them, and re-layouts: 172 us -> 12.2 us
  matrix products: 111 us -> 15.9 us
  other arithmetic: 49.8 us -> 6.54 us
  between operations: 15.3 us -> 0.37 us
    pallas_call x0 -> x6, Pallas kernels: none -> 391 us  [the longest x1 265 us: gather_all(): pl.pallas_call(gather_kernel, out_shape=(jax.ShapeDtypeStruct((64, 1, 128...]
    all_gather x5 -> x0, waiting for transfers between devices: 290 us -> none  [the longest x1 82.3 us: body(): stream_all = lax.all_gather(stream_own, 'tensor', axis=0, tiled=True)]
    reduce_scatter x2 -> x0, waiting for transfers between devices: 129 us -> none  [the longest x1 81.1 us: body(): lax.psum_scatter(jnp.dot(hyena_mix, hyena_out, preferred_element_type=jnp...]
    gather x4 -> x0, local copies, waits for them, and re-layouts: 122 us -> none  [the longest x2 61.2 us: toeplitz(): jnp.take(long_filter, jnp.clip(tap_lag + filter_len, 0, filter_len - 1),...]
    dot_general x75 -> x2, matrix products: 111 us -> 15.9 us  [the longest x1 9.52 us: body(): return stream_own + jnp.dot(att, wa, preferred_element_type=F32)]
    reduce_sum x51 -> x4, other arithmetic: 26.1 us -> 1.85 us  [the longest x1 0.84 us: body(): jnp.sum(jnp.where(slot_ids[None] == pair[:, None], block_order[None], 0),...]
    dynamic_slice x16 -> x1, local copies, waits for them, and re-layouts: 20.4 us -> 0.01 us  [body(): own_ids = lax.dynamic_slice_in_dim(ids_blocks, 2 * ctx, 2, 0)]
    slice x32 -> x4, local copies, waits for them, and re-layouts: 21 us -> 1.16 us  [the longest x1 1.06 us: body(): embed[c:c + 1]]
  transfers between devices with their start and end apart: 7 -> 0, of which waited for: 6 -> 0; matrix products, arithmetic and copies ran while one was open for 17% -> 0% of each run, Pallas kernels for 0% -> 0%
where the time goes in v1:
time: 426 us
  Pallas kernels  391 us (92%)
  matrix products  15.9 us (4%)
  local copies, waits for them, and re-layouts  12.2 us (3%)
  other arithmetic  6.54 us (2%)
    pallas_call x1, Pallas kernels, gather_all(): pl.pallas_call(gather_kernel, out_shape=(jax.ShapeDtypeStruct((64, 1, 128...  265 us
    pallas_call x1, Pallas kernels, exchange(): pl.pallas_call(exchange_kernel, out_shape=(jax.ShapeDtypeStruct((16, 2, 6...  36.5 us
    pallas_call x1, Pallas kernels, attend(): pl.pallas_call(attend_kernel, out_shape=jax.ShapeDtypeStruct((32, 64, 128...  34.2 us
    pallas_call x1, Pallas kernels, stream_qkv(): pl.pallas_call(proj_kernel, out_shape=(jax.ShapeDtypeStruct((128, 4096),...  24.7 us
    pallas_call x1, Pallas kernels, hyena_mix(): pl.pallas_call(mix_kernel, out_shape=jax.ShapeDtypeStruct((512, 2048), BF...  16.1 us
    pallas_call x1, Pallas kernels, give_back(): pl.pallas_call(return_kernel, out_shape=jax.ShapeDtypeStruct((32, 64, 128...  14.3 us
    dot_general x1, matrix products, body(): return stream_own + jnp.dot(att, wa, preferred_element_type=F32)  9.52 us

profile of v1, /device:TPU:1, one launch (start us, length us, event | category | flops | bytes accessed | tf_op | source)
XLA Modules:
  0.0 425.6 jit_solution(1379035855619884074)
XLA Ops:
  0.0 0.8 fusion.11
  0.8 0.8 select_reduce_fusion.1
  1.6 0.1 pad_add_fusion.1.slot_ref
  1.7 0.1 pad.11.clone
  1.8 0.7 broadcast_compare_fusion.1
  2.5 0.1 convert_bitcast_fusion
  2.6 1.1 fusion.12
  3.7 0.4 concatenate.35.emb_ref
  4.1 0.1 fusion.1
  4.3 0.0 copy-start.6
  4.3 0.0 copy-start.7
  4.3 0.0 copy-start.8
  4.3 6.4 %fusion = bf16[3,16,512]{2,1,0:T(8,128)(2,1)S(1)} fusion(bf16[3,4096,512]{2,1,0:T(8,128)(2,1)} %param.17, bf16[16,4096]{1,0:T(8,128)(2,1)S(1)} %concatenate.35.emb_ref, f32[4096]{0:T(1024)} %param.16, f32[16]{0:T(128)S(1)} %add_rsqrt_fusion), kind=kOutput, calls=%fused_computation.2 | convolution fusion | flops 201613312 | bytes 12779584 | tf_op jit(solution)/shard_map/rd,jdc->jrc/dot_general | solution.py:601
  10.7 0.0 copy-done.6
  10.8 0.0 copy-done.7
  10.8 0.0 copy-done.8
  10.8 0.6 maximum_bitcast_fusion.pack_ref
  11.4 1.0 fusion.8
  12.4 0.2 pad_maximum_fusion
  12.7 0.0 copy-start.9
  12.7 264.7 %gather_all.1 = (s32[64,1,128]{2,1,0:T(1,128)}, f32[4,180,128]{2,1,0:T(8,128)}, bf16[2048,4096]{1,0:T(8,128)(2,1)}, bf16[2048,4096]{1,0:T(8,128)(2,1)}) custom-call(s32[1,1,128]{2,1,0:T(1,128)} %bitcast.53, f32[180,128]{1,0:T(8,128)} %maximum_bitcast_fusion.pack_ref, bf16[512,4096]{1,0:T(8,128)(2,1)} %wh_ref.1, bf16[512,4096]{1,0:T(8,128)(2,1)} %wa_ref.1), custom_call_target="tpu_custom_call" | custom-call | tf_op jit(solution)/shard_map/gather_all/pallas_call | solution.py:205
  277.4 0.5 broadcast.107
  277.9 1.5 reduce.3
  279.4 0.0 copy-start.5
  279.4 1.1 copy.29
  280.6 0.1 slice.49
  280.6 0.1 select_reduce_fusion
  280.7 0.1 pad_add_fusion
  280.9 0.0 copy-done.9
  280.9 0.1 compare_convert_fusion
  281.0 0.1 concatenate.38
  281.1 0.1 broadcast_compare_fusion
  281.4 0.1 rev.3
  281.4 0.1 maximum_maximum_fusion.taps_ref
  281.6 0.2 reshape.145
  281.8 0.2 copy.20
  282.0 0.2 reshape.146
  282.2 0.2 copy.21.onehot_ref
  282.4 16.1 %hyena_mix.1.mix_ref = bf16[512,2048]{1,0:T(8,128)(2,1)S(1)} custom-call(bf16[768,32]{1,0:T(8,128)(2,1)S(1)} %copy.21.onehot_ref, f32[3,16,2048]{2,1,0:T(8,128)S(1)} %concatenate.39.tab_ref, f32[128,256]{1,0:T(8,128)S(1)} %maximum_maximum_fusion.taps_ref, f32[1,2048]{1,0:T(1,128)S(1)} %bitcast.39), custom_call_target="tpu_custom_call" | custom-call | tf_op jit(solution)/shard_map/hyena_mix/pallas_call | solution.py:251
  298.5 0.0 copy-start
  298.5 1.3 copy-done
  299.9 0.0 copy-done.5
  299.9 24.7 %stream_qkv.1 = (f32[128,4096]{1,0:T(8,128)S(1)}, bf16[4,3,2,4,64,128]{5,4,3,2,1,0:T(8,128)(2,1)S(1)}) custom-call(s32[1]{0:T(128)} %bitcast.t_ref, bf16[512,2048]{1,0:T(8,128)(2,1)} %copy-done, bf16[2048,4096]{1,0:T(8,128)(2,1)} %get-tuple-element.15.wh_ref, bf16[512,16]{1,0:T(8,128)(2,1)S(1)} %pad_convert_fusion.code_ref, ...), custom_call_target="tpu_custom_call" | custom-call | tf_op jit(solution)/shard_map/stream_qkv/pallas_call | solution.py:313
  324.6 0.0 copy-start.3
  324.6 1.1 copy-done.3
  325.7 36.5 %exchange.1 = (bf16[16,2,64,128]{3,2,1,0:T(8,128)(2,1)}, bf16[16,2,2,4,64,128]{5,4,3,2,1,0:T(8,128)(2,1)}) custom-call(bf16[4,3,2,4,64,128]{5,4,3,2,1,0:T(8,128)(2,1)} %copy-done.3), custom_call_target="tpu_custom_call" | custom-call | tf_op jit(solution)/shard_map/exchange/pallas_call | solution.py:422
  362.3 0.0 copy-start.1
  362.3 2.2 copy-done.1
  364.4 0.0 copy-start.4
  364.4 1.0 copy-done.4
  365.5 34.2 %attend.1.o_ref = bf16[32,64,128]{2,1,0:T(8,128)(2,1)S(1)} custom-call(s32[33]{0:T(128)S(1)} %pad_add_fusion.1.slot_ref, bf16[16,2,64,128]{3,2,1,0:T(8,128)(2,1)S(1)} %copy-done.4, bf16[16,2,2,256,128]{4,3,2,1,0:T(8,128)(2,1)S(1)} %bitcast.38), custom_call_target="tpu_custom_call" | custom-call | tf_op jit(solution)/shard_map/attend/pallas_call | solution.py:490
  399.6 0.0 copy-start.2
  399.7 0.8 copy-done.2
  400.4 14.3 %give_back.1 = bf16[32,64,128]{2,1,0:T(8,128)(2,1)} custom-call(bf16[32,64,128]{2,1,0:T(8,128)(2,1)} %copy-done.2), custom_call_target="tpu_custom_call" | custom-call | tf_op jit(solution)/shard_map/give_back/pallas_call | solution.py:582
  414.8 1.3 copy.22
  416.1 9.5 %convolution_add_fusion = f32[128,4096]{1,0:T(8,128)} fusion(f32[128,4096]{1,0:T(8,128)S(1)} %get-tuple-element.16, bf16[128,2048]{0,1:T(8,128)(2,1)S(1)} %bitcast.41, bf16[2048,4096]{1,0:T(8,128)(2,1)} %get-tuple-element.20), kind=kOutput, calls=%fused_computation | convolution fusion | flops 2148007936 | bytes 21495808 | tf_op jit(solution)/shard_map/dot_general | solution.py:650
  (26 shorter events, 0.3 us)
Async XLA Ops:
  4.3 6.4 %copy-start.6 = (f32[3,3,512]{2,1,0:T(4,128)S(1)}, f32[3,3,512]{2,1,0:T(4,128)}, u32[]{:S(2)}) copy-start(f32[3,3,512]{2,1,0:T(4,128)} %param.18) | copy-start | bytes 55300
  4.3 6.5 %copy-start.7 = (f32[32,128]{1,0:T(8,128)S(1)}, f32[32,128]{1,0:T(8,128)}, u32[]{:S(2)}) copy-start(f32[32,128]{1,0:T(8,128)} %param.19) | copy-start | bytes 49156
  4.3 6.5 %copy-start.8 = (f32[512]{0:T(512)S(1)}, f32[512]{0:T(512)}, u32[]{:S(2)}) copy-start(f32[512]{0:T(512)} %param.20) | copy-start | bytes 6148
  12.7 268.2 %copy-start.9 = (s32[4]{0:T(128)S(1)}, s32[4]{0:T(128)}, u32[]{:S(2)}) copy-start(s32[4]{0:T(128)} %constant.74.clone) | copy-start | bytes 52
  279.4 20.4 %copy-start.5 = (f32[4096]{0:T(1024)S(1)}, f32[4096]{0:T(1024)}, u32[]{:S(2)}) copy-start(f32[4096]{0:T(1024)} %param.22) | copy-start | bytes 49156
  298.5 1.3 copy-start
  324.6 1.1 copy-start.3
  362.3 2.2 copy-start.1
  364.4 1.0 copy-start.4
  399.6 0.8 copy-start.2

commit v2 on v1

--- a/solution.py
+++ b/solution.py
@@ -40,8 +40,9 @@
 
 
 class WeightGather:
-    def __init__(self, w_in, w_out, send, recv, local_sem):
-        self.w_in, self.w_out, self.send, self.recv, self.local_sem = w_in, w_out, send, recv, local_sem
+    def __init__(self, w_in, w_out, send, recv, hold, local_sem):
+        self.w_in, self.w_out, self.send, self.recv = w_in, w_out, send, recv
+        self.hold, self.local_sem = hold, local_sem
         dp, y, x, t = coords()
         self.dp, self.t = dp, t
         u, w = pick(dp, x, y), pick(dp, y, x)
@@ -77,9 +78,8 @@
         remote(dst, dst, self.send.at[0], self.recv.at[recv_at], self.sib).wait_recv()
 
     def start(self):
-        row = pl.multiple_of(self.t * self.shard, self.shard)
-        self.local = pltpu.make_async_copy(self.w_in, self.w_out.at[pl.ds(row, self.shard), :], self.local_sem)
-        self.local.start()
+        self.load = pltpu.make_async_copy(self.w_in, self.hold, self.local_sem.at[0])
+        self.load.start()
         for h in (0, 1):
             dst = self.unit(self.t, self.dp, self.q, h)
             first, second = ((self.zp, 0 + h), (self.zm, 2 + h))
@@ -89,6 +89,12 @@
             else:
                 self.go(self.own(1), dst, 1, self.zp)
                 self.go(self.own(0), self.unit(self.t, self.dp, self.q, 0), 2, self.zm)
+
+    def keep(self):
+        row = pl.multiple_of(self.t * self.shard, self.shard)
+        self.load.wait()
+        self.local = pltpu.make_async_copy(self.hold, self.w_out.at[pl.ds(row, self.shard), :], self.local_sem.at[1])
+        self.local.start()
 
     def z_step(self, kind):
         zoff, h = ZKINDS[kind]
@@ -129,8 +135,8 @@
 N_SENDS = 6 + 18 + 24
 
 
-def gather_kernel(ids_ref, pack_ref, wh_ref, wa_ref, ids_out, pack_out, wh_out, wa_out,
-                  sh, rh, sa, ra, s_ids, r_ids, s_pack, r_pack, loc):
+def gather_kernel(ids_ref, pack_ref, wh_ref, wa_ref, ids_out, pack_out, wh_out,
+                  sh, rh, sa, ra, s_ids, r_ids, s_pack, r_pack, hold_h, hold_a, loc_h, loc_a, loc):
     dp, y, x, t = coords()
     ctx = y * 4 + x
     barrier = pltpu.get_barrier_semaphore()
@@ -146,9 +152,9 @@
 
     small = []
     mine = ctx * 4 + t
-    keep_ids = pltpu.make_async_copy(ids_ref, ids_out.at[pl.ds(mine, 1)], loc.at[2])
+    keep_ids = pltpu.make_async_copy(ids_ref, ids_out.at[pl.ds(mine, 1)], loc.at[0])
     keep_ids.start()
-    keep_pack = pltpu.make_async_copy(pack_ref, pack_out.at[t], loc.at[3])
+    keep_pack = pltpu.make_async_copy(pack_ref, pack_out.at[t], loc.at[1])
     keep_pack.start()
     for d in (1, 2, 3):
         c = remote(ids_ref, ids_out.at[pl.ds(mine, 1)], s_ids.at[d - 1], r_ids.at[d - 1], partners[d - 1])
@@ -157,8 +163,7 @@
         c = remote(pack_ref, pack_out.at[t], s_pack.at[d - 1], r_pack.at[d - 1], partners[d - 1])
         c.start()
         small.append(c)
-    gh = WeightGather(wh_ref, wh_out, sh, rh, loc.at[0])
-    ga = WeightGather(wa_ref, wa_out, sa, ra, loc.at[1])
+    gh = WeightGather(wh_ref, wh_out, sh, rh, hold_h, loc_h)
     gh.start()
     keep_ids.wait()
     for d in (1, 2, 3):
@@ -179,17 +184,11 @@
         small.append(c)
     for k in KIND_ORDER:
         gh.z_step(k)
-    ga.start()
+    gh.keep()
     for k in KIND_ORDER:
         for side in range(3):
             gh.plane_step(side, k)
-    for k in KIND_ORDER:
-        ga.z_step(k)
     gh.finish()
-    for k in KIND_ORDER:
-        for side in range(3):
-            ga.plane_step(side, k)
-    ga.finish()
     for d in (1, 2, 3):
         ref = ids_out.at[pl.ds(((y + 4 - d) % 4) * 16, 16)]
         remote(ref, ref, s_ids.at[0], r_ids.at[5 + d], partners[0]).wait_recv()
@@ -208,15 +207,17 @@
             jax.ShapeDtypeStruct((64, 1, 128), jnp.int32),
             jax.ShapeDtypeStruct((4,) + pack.shape, F32),
             jax.ShapeDtypeStruct((2048, 4096), BF16),
-            jax.ShapeDtypeStruct((2048, 4096), BF16),
         ),
         in_specs=[ANY] * 4,
-        out_specs=(ANY,) * 4,
+        out_specs=(ANY,) * 3,
         scratch_shapes=[
             dma((N_SENDS,)), dma((48,)), dma((N_SENDS,)), dma((48,)),
-            dma((9,)), dma((9,)), dma((3,)), dma((3,)), dma((4,)),
+            dma((9,)), dma((9,)), dma((3,)), dma((3,)),
+            pltpu.VMEM(wh.shape, BF16), pltpu.VMEM(wa.shape, BF16), dma((2,)), dma((2,)), dma((2,)),
         ],
-        compiler_params=pltpu.CompilerParams(collective_id=0, has_side_effects=True),
+        compiler_params=pltpu.CompilerParams(
+            collective_id=0, has_side_effects=True, vmem_limit_bytes=32 * 2**20
+        ),
         name="gather_all",
     )(ids, pack, wh, wa)
 
@@ -603,7 +604,8 @@
     pack = jnp.concatenate(
         [table.reshape(-1), long_filter.reshape(-1), conv_skip.reshape(-1)]
     ).reshape(-1, 128)
-    ids_all, packs, wh, wa = gather_all(ids.reshape(1, 1, 128), pack, hyena_out, attn_out)
+    ids_all, packs, wh = gather_all(ids.reshape(1, 1, 128), pack, hyena_out, attn_out)
+    wa = lax.all_gather(lax.dynamic_slice_in_dim(attn_out, (dp * 16 + ctx) * 16, 16, 0), ("tensor", "dp", "context"), axis=0, tiled=True)
 
     packs = packs.reshape(4, -1)
     n_tab = 36 * 512

time: 426 us -> 229 us (0.54)
  Pallas kernels: 391 us -> 182 us
  between operations: 0.37 us -> 13.8 us
    pallas_call x1, Pallas kernels: 265 us -> 59.3 us  [gather_all(): pl.pallas_call(gather_kernel, out_shape=(jax.ShapeDtypeStruct((64, 1, 128...]
  transfers between devices with their start and end apart: 0 -> 1, of which waited for: 0 -> 0; matrix products, arithmetic and copies ran while one was open for 0% -> 6% of each run, Pallas kernels for 0% -> 80%
where the time goes in v2:
time: 229 us
  Pallas kernels  182 us (79%)
  matrix products  16 us (7%)
  between operations  13.8 us (6%)
  local copies, waits for them, and re-layouts  13.2 us (6%)
  other arithmetic  3.17 us (1%)
    pallas_call x1, Pallas kernels, gather_all(): pl.pallas_call(gather_kernel, out_shape=(jax.ShapeDtypeStruct((64, 1, 128...  59.3 us
    pallas_call x1, Pallas kernels, attend(): pl.pallas_call(attend_kernel, out_shape=jax.ShapeDtypeStruct((32, 64, 128...  34.1 us
    pallas_call x1, Pallas kernels, exchange(): pl.pallas_call(exchange_kernel, out_shape=(jax.ShapeDtypeStruct((16, 2, 6...  33.1 us
    pallas_call x1, Pallas kernels, stream_qkv(): pl.pallas_call(proj_kernel, out_shape=(jax.ShapeDtypeStruct((128, 4096),...  24.6 us
    pallas_call x1, Pallas kernels, hyena_mix(): pl.pallas_call(mix_kernel, out_shape=jax.ShapeDtypeStruct((512, 2048), BF...  16.1 us
    pallas_call x1, Pallas kernels, give_back(): pl.pallas_call(return_kernel, out_shape=jax.ShapeDtypeStruct((32, 64, 128...  15.2 us
    dot_general x1, matrix products, body(): return stream_own + jnp.dot(att, wa, preferred_element_type=F32)  9.5 us
    unnamed x35, local copies, waits for them, and re-layouts  7.08 us
  transfers between devices with their start and end apart: 1, of which 0 were waited for; matrix products, arithmetic and copies ran while one was open for 6% of the time, Pallas kernels for 80%

profile of v2, /device:TPU:1, one launch (start us, length us, event | category | flops | bytes accessed | tf_op | source)
XLA Modules:
  0.0 228.7 jit_solution(4817030401396165505)
XLA Ops:
  6.5 0.0 all-gather.2.cloned.1.call-start
  6.5 1.6 constant_dynamic-slice_fusion
  8.1 0.0 all-gather.2.cloned.1.call-update
  8.1 1.1 fusion.12
  9.2 0.4 concatenate.35.emb_ref
  9.7 0.1 fusion.1
  9.8 0.0 copy-start.9
  9.8 0.0 copy-start.10
  9.8 0.0 copy-start.11
  9.8 0.0 copy-start.1
  9.9 0.0 copy-start.2
  9.9 0.0 copy-start.8
  9.9 6.5 %fusion = bf16[3,16,512]{2,1,0:T(8,128)(2,1)S(1)} fusion(bf16[3,4096,512]{2,1,0:T(8,128)(2,1)} %param.17, bf16[16,4096]{1,0:T(8,128)(2,1)S(1)} %concatenate.35.emb_ref, f32[4096]{0:T(1024)} %param.16, f32[16]{0:T(128)S(1)} %add_rsqrt_fusion), kind=kOutput, calls=%fused_computation.2 | convolution fusion | flops 201613312 | bytes 12779584 | tf_op jit(solution)/shard_map/rd,jdc->jrc/dot_general | solution.py:602
  16.4 0.0 copy-done.9
  16.5 0.0 copy-done.10
  16.5 0.0 copy-done.11
  16.5 0.0 copy-done.1
  16.5 0.4 copy-done.2
  16.9 0.0 copy-done.8
  16.9 0.0 copy-start.13
  16.9 59.3 %gather_all.1 = (s32[64,1,128]{2,1,0:T(1,128)S(1)}, f32[4,180,128]{2,1,0:T(8,128)S(1)}, bf16[2048,4096]{1,0:T(8,128)(2,1)}) custom-call(s32[1,1,128]{2,1,0:T(1,128)S(1)} %bitcast.42, f32[180,128]{1,0:T(8,128)S(1)} %maximum_bitcast_fusion.pack_ref, bf16[512,4096]{1,0:T(8,128)(2,1)S(1)} %copy-done.2, bf16[512,4096]{1,0:T(8,128)(2,1)S(1)} %copy-done.1), custom_call_target="tpu_custom_call" | custom-call | tf_op jit(solution)/shard_map/gather_all/pallas_call | solution.py:204
  76.3 0.1 copy.29
  76.4 0.5 broadcast.107
  77.0 0.7 reduce.3
  77.7 0.1 slice.49
  77.8 0.0 copy-done.13
  77.8 0.2 fusion.11
  78.0 0.1 broadcast_compare_fusion.1
  78.1 0.1 select_reduce_fusion
  78.2 0.1 pad_add_fusion
  78.3 0.0 copy-done.12
  78.3 0.1 compare_convert_fusion
  78.4 0.1 concatenate.38
  78.5 0.2 copy.21.onehot_ref
  78.6 0.0 copy-start.7
  78.6 0.2 reshape.145
  78.9 0.2 copy.20
  79.1 0.2 reshape.146
  79.3 0.1 rev.3
  79.5 0.1 pad.11.clone
  79.6 0.1 convert_bitcast_fusion
  79.7 0.1 maximum_maximum_fusion.taps_ref
  79.8 16.1 %hyena_mix.1.mix_ref = bf16[512,2048]{1,0:T(8,128)(2,1)S(1)} custom-call(bf16[768,32]{1,0:T(8,128)(2,1)S(1)} %copy.21.onehot_ref, f32[3,16,2048]{2,1,0:T(8,128)S(1)} %concatenate.39.tab_ref, f32[128,256]{1,0:T(8,128)S(1)} %maximum_maximum_fusion.taps_ref, f32[1,2048]{1,0:T(1,128)S(1)} %bitcast.40), custom_call_target="tpu_custom_call" | custom-call | tf_op jit(solution)/shard_map/hyena_mix/pallas_call | solution.py:252
  95.9 0.0 copy-start
  95.9 1.3 copy-done
  97.2 0.1 broadcast_compare_fusion
  97.4 1.0 fusion.8
  98.4 0.2 pad_maximum_fusion
  98.6 0.0 copy-done.7
  98.7 24.6 %stream_qkv.1 = (f32[128,4096]{1,0:T(8,128)S(1)}, bf16[4,3,2,4,64,128]{5,4,3,2,1,0:T(8,128)(2,1)S(1)}) custom-call(s32[1]{0:T(128)} %bitcast.t_ref, bf16[512,2048]{1,0:T(8,128)(2,1)} %copy-done, bf16[2048,4096]{1,0:T(8,128)(2,1)} %get-tuple-element.14.wh_ref, bf16[512,16]{1,0:T(8,128)(2,1)S(1)} %pad_convert_fusion.code_ref, ...), custom_call_target="tpu_custom_call" | custom-call | tf_op jit(solution)/shard_map/stream_qkv/pallas_call | solution.py:314
  123.3 0.0 copy-start.5
  123.3 1.1 copy-done.5
  124.4 33.1 %exchange.1 = (bf16[16,2,64,128]{3,2,1,0:T(8,128)(2,1)}, bf16[16,2,2,4,64,128]{5,4,3,2,1,0:T(8,128)(2,1)}) custom-call(bf16[4,3,2,4,64,128]{5,4,3,2,1,0:T(8,128)(2,1)} %copy-done.5), custom_call_target="tpu_custom_call" | custom-call | tf_op jit(solution)/shard_map/exchange/pallas_call | solution.py:423
  157.5 0.1 select_reduce_fusion.1
  157.6 0.1 pad_add_fusion.1.slot_ref
  157.7 2.2 copy-done.3
  159.9 1.0 copy-done.6
  160.9 34.1 %attend.1.o_ref = bf16[32,64,128]{2,1,0:T(8,128)(2,1)S(1)} custom-call(s32[33]{0:T(128)S(1)} %pad_add_fusion.1.slot_ref, bf16[16,2,64,128]{3,2,1,0:T(8,128)(2,1)S(1)} %copy-done.6, bf16[16,2,2,256,128]{4,3,2,1,0:T(8,128)(2,1)S(1)} %bitcast.38), custom_call_target="tpu_custom_call" | custom-call | tf_op jit(solution)/shard_map/attend/pallas_call | solution.py:491
  195.0 0.0 copy-start.4
  195.1 0.8 copy-done.4
  195.8 15.2 %give_back.1 = bf16[32,64,128]{2,1,0:T(8,128)(2,1)} custom-call(bf16[32,64,128]{2,1,0:T(8,128)(2,1)} %copy-done.4), custom_call_target="tpu_custom_call" | custom-call | tf_op jit(solution)/shard_map/give_back/pallas_call | solution.py:583
  211.0 1.3 copy.22
  212.4 0.0 all-gather.2.cloned.1.call-done
  212.4 9.5 %convolution_add_fusion = f32[128,4096]{1,0:T(8,128)} fusion(f32[128,4096]{1,0:T(8,128)S(1)} %get-tuple-element.15, bf16[128,2048]{0,1:T(8,128)(2,1)S(1)} %bitcast.43, bf16[2048,4096]{1,0:T(8,128)(2,1)} %all-gather.2.cloned.1.call-done), kind=kOutput, calls=%fused_computation | convolution fusion | flops 2148007936 | bytes 21495808 | tf_op jit(solution)/shard_map/dot_general | solution.py:652
  (30 shorter events, 0.3 us)
Async XLA Ops:
  6.5 205.9 %all-gather.2.cloned.1.call-start = ((), (), s32[]{:S(2)}) async-start(), calls=%async_computation | async-start | bytes 16908288 | tf_op jit(solution)/shard_map/all_gather | solution.py:608
  9.8 6.6 %copy-start.9 = (f32[3,3,512]{2,1,0:T(4,128)S(1)}, f32[3,3,512]{2,1,0:T(4,128)}, u32[]{:S(2)}) copy-start(f32[3,3,512]{2,1,0:T(4,128)} %param.18) | copy-start | bytes 55300
  9.8 6.7 %copy-start.10 = (f32[32,128]{1,0:T(8,128)S(1)}, f32[32,128]{1,0:T(8,128)}, u32[]{:S(2)}) copy-start(f32[32,128]{1,0:T(8,128)} %param.19) | copy-start | bytes 49156
  9.8 6.7 %copy-start.11 = (f32[512]{0:T(512)S(1)}, f32[512]{0:T(512)}, u32[]{:S(2)}) copy-start(f32[512]{0:T(512)} %param.20) | copy-start | bytes 6148
  9.8 6.7 %copy-start.1 = (bf16[512,4096]{1,0:T(8,128)(2,1)S(1)}, bf16[512,4096]{1,0:T(8,128)(2,1)}, u32[]{:S(2)}) copy-start(bf16[512,4096]{1,0:T(8,128)(2,1)} %wa_ref.1) | copy-start | bytes 12582916
  9.9 7.1 %copy-start.2 = (bf16[512,4096]{1,0:T(8,128)(2,1)S(1)}, bf16[512,4096]{1,0:T(8,128)(2,1)}, u32[]{:S(2)}) copy-start(bf16[512,4096]{1,0:T(8,128)(2,1)} %wh_ref.1) | copy-start | bytes 12582916
  9.9 7.1 %copy-start.8 = (s32[128]{0:T(128)S(1)}, s32[128]{0:T(128)}, u32[]{:S(2)}) copy-start(s32[128]{0:T(128)} %param.13) | copy-start | bytes 1540
  16.9 60.9 %copy-start.13 = (s32[32]{0:T(128)S(1)}, s32[32]{0:T(128)}, u32[]{:S(2)}) copy-start(s32[32]{0:T(128)} %param.14) | copy-start | bytes 388
  16.9 61.3 %copy-start.12 = (s32[4]{0:T(128)S(1)}, s32[4]{0:T(128)}, u32[]{:S(2)}) copy-start(s32[4]{0:T(128)} %constant.78.clone) | copy-start | bytes 52
  78.6 20.0 %copy-start.7 = (f32[4096]{0:T(1024)S(1)}, f32[4096]{0:T(1024)}, u32[]{:S(2)}) copy-start(f32[4096]{0:T(1024)} %param.22) | copy-start | bytes 49156
  95.9 1.3 copy-start
  123.3 1.1 copy-start.5
  157.7 2.2 copy-start.3
  159.9 1.0 copy-start.6
  195.0 0.8 copy-start.4
Sparse Core Ops, SparseCore 0:
  10.5 87.5 all-gather.1

commit v3 on v2

--- a/solution.py
+++ b/solution.py
@@ -135,134 +135,164 @@
 N_SENDS = 6 + 18 + 24
 
 
-def gather_kernel(ids_ref, pack_ref, wh_ref, wa_ref, ids_out, pack_out, wh_out,
-                  sh, rh, sa, ra, s_ids, r_ids, s_pack, r_pack, hold_h, hold_a, loc_h, loc_a, loc):
+def code_rows(shape):
+    k = lax.broadcasted_iota(jnp.int32, shape, 0) % 4
+    return jnp.where(k < 2, jnp.where(k == 0, CODES[0], CODES[1]), jnp.where(k == 2, CODES[2], CODES[3]))
+
+
+def hyena_kernel(ids_ref, hit_ref, emb_ref, gain_ref, proj_ref, short_ref, taps_ref, skip_ref, wh_ref,
+                 mix_ref, hot_out, wh_out,
+                 ids_all, tab_all, taps_all, hots, proj_s, hold,
+                 s_w, r_w, loc_w, s_ids, r_ids, s_tab, r_tab, s_taps, r_taps, p_sem):
     dp, y, x, t = coords()
     ctx = y * 4 + x
+    loads = [pltpu.make_async_copy(proj_ref.at[j], proj_s.at[j], p_sem.at[j]) for j in range(3)]
+    for c in loads:
+        c.start()
     barrier = pltpu.get_barrier_semaphore()
-    partners = (
-        [{"tensor": (t + d) % 4} for d in (1, 2, 3)]
-        + [{"context": y * 4 + (x + d) % 4} for d in (1, 2, 3)]
-        + [{"context": ((y + d) % 4) * 4 + x} for d in (1, 2, 3)]
-        + [{"dp": 1 - dp}]
-    )
+    zs = [{"tensor": (t + d) % 4} for d in (1, 2, 3)]
+    xs = [{"context": y * 4 + (x + d) % 4} for d in (1, 2, 3)]
+    ys = [{"context": ((y + d) % 4) * 4 + x} for d in (1, 2, 3)]
+    partners = zs + xs + ys + [{"dp": 1 - dp}]
     for where in partners:
         pl.semaphore_signal(barrier, inc=1, device_id=where, device_id_type=MESH_ID)
+    mine = ctx * 4 + t
+    ids_all[mine] = ids_ref[...]
+    trow = pl.ds(pl.multiple_of(t * 32, 32), 32)
+    taps_all[trow, :] = taps_ref[...]
     pl.semaphore_wait(barrier, len(partners))
 
     small = []
-    mine = ctx * 4 + t
-    keep_ids = pltpu.make_async_copy(ids_ref, ids_out.at[pl.ds(mine, 1)], loc.at[0])
-    keep_ids.start()
-    keep_pack = pltpu.make_async_copy(pack_ref, pack_out.at[t], loc.at[1])
-    keep_pack.start()
-    for d in (1, 2, 3):
-        c = remote(ids_ref, ids_out.at[pl.ds(mine, 1)], s_ids.at[d - 1], r_ids.at[d - 1], partners[d - 1])
+
+    def go(src, send, recv, where):
+        c = remote(src, src, send, recv, where)
         c.start()
         small.append(c)
-        c = remote(pack_ref, pack_out.at[t], s_pack.at[d - 1], r_pack.at[d - 1], partners[d - 1])
-        c.start()
-        small.append(c)
-    gh = WeightGather(wh_ref, wh_out, sh, rh, hold_h, loc_h)
+
+    def landed(ref, recv):
+        remote(ref, ref, s_ids.at[0], recv, zs[0]).wait_recv()
+
+    gh = WeightGather(wh_ref, wh_out, s_w, r_w, hold, loc_w)
+    for d in (0, 1, 2):
+        go(ids_all.at[pl.ds(mine, 1)], s_ids.at[d], r_ids.at[d], zs[d])
     gh.start()
-    keep_ids.wait()
-    for d in (1, 2, 3):
-        ref = ids_out.at[pl.ds(ctx * 4 + (t + 4 - d) % 4, 1)]
-        remote(ref, ref, s_ids.at[0], r_ids.at[d - 1], partners[0]).wait_recv()
-    row = ids_out.at[pl.ds(ctx * 4, 4)]
-    for d in (1, 2, 3):
-        c = remote(row, row, s_ids.at[2 + d], r_ids.at[2 + d], partners[2 + d])
-        c.start()
-        small.append(c)
-    for d in (1, 2, 3):
-        ref = ids_out.at[pl.ds((y * 4 + (x + 4 - d) % 4) * 4, 4)]
-        remote(ref, ref, s_ids.at[0], r_ids.at[2 + d], partners[0]).wait_recv()
-    row = ids_out.at[pl.ds(y * 16, 16)]
-    for d in (1, 2, 3):
-        c = remote(row, row, s_ids.at[5 + d], r_ids.at[5 + d], partners[5 + d])
-        c.start()
-        small.append(c)
-    for k in KIND_ORDER:
-        gh.z_step(k)
+    for d in (0, 1, 2):
+        go(taps_all.at[trow, :], s_taps.at[d], r_taps.at[d], zs[d])
+
+    wide = emb_ref[...].astype(F32)
+    square = jnp.sum(wide * wide, axis=1, keepdims=True)
+    normed = (wide * lax.rsqrt(square / 4096.0 + EPS) * gain_ref[...]).astype(BF16)
+    cols = pl.ds(pl.multiple_of(t * 512, 512), 512)
+    for j in range(3):
+        loads[j].wait()
+        rows = jnp.dot(normed, proj_s[j], preferred_element_type=F32).astype(BF16).astype(F32)[0:4]
+        last = jnp.broadcast_to(skip_ref[...], (4, 512))
+        tab_all[j, :, cols] = jnp.concatenate([short_ref[j, tap : tap + 1, :] * rows for tap in range(3)] + [last], axis=0)
+    for d in (0, 1, 2):
+        go(tab_all.at[:, :, cols], s_tab.at[d], r_tab.at[d], zs[d])
+    for d in (0, 1, 2):
+        landed(ids_all.at[pl.ds(ctx * 4 + (t + 3 - d) % 4, 1)], r_ids.at[d])
+    for d in (0, 1, 2):
+        go(ids_all.at[pl.ds(ctx * 4, 4)], s_ids.at[3 + d], r_ids.at[3 + d], xs[d])
+    gh.z_step(0)
+    gh.z_step(3)
+    for d in (0, 1, 2):
+        landed(ids_all.at[pl.ds((y * 4 + (x + 3 - d) % 4) * 4, 4)], r_ids.at[3 + d])
+    for d in (0, 1, 2):
+        go(ids_all.at[pl.ds(y * 16, 16)], s_ids.at[6 + d], r_ids.at[6 + d], ys[d])
+    gh.z_step(1)
+    gh.z_step(2)
     gh.keep()
-    for k in KIND_ORDER:
+    for d in (0, 1, 2):
+        landed(ids_all.at[pl.ds(((y + 3 - d) % 4) * 16, 16)], r_ids.at[6 + d])
+        zrow = pl.ds(pl.multiple_of(((t + 3 - d) % 4) * 32, 32), 32)
+        landed(taps_all.at[zrow, :], r_taps.at[d])
+        landed(tab_all.at[:, :, pl.ds(pl.multiple_of(((t + 3 - d) % 4) * 512, 512), 512)], r_tab.at[d])
+
+    row8 = lax.broadcasted_iota(jnp.int32, (8, 384), 0)
+    code8 = code_rows((8, 384))
+    for b in range(2):
+        prev = [jnp.zeros((8, 128), jnp.int32) for _ in range(2)]
+        for slot in range(32):
+            hit = hit_ref[b * 32 + slot]
+            for half in range(2):
+                prev[half] = prev[half] + hit * ids_all[2 * slot + half]
+        own = [ids_all[ctx * 4 + 2 * b + half] for half in range(2)]
+        line = jnp.concatenate(prev + own, axis=1)
+        back = [line[:, 128:]] + [pltpu.roll(line, tap, 1)[:, 128:] for tap in (1, 2)]
+        top = jnp.where(jnp.where(row8 < 4, back[0], back[1]) == code8, 1.0, 0.0)
+        low = jnp.where(row8 < 4, jnp.where(back[2] == code8, 1.0, 0.0), 0.0)
+        hots[b * 384 : (b + 1) * 384, :] = jnp.concatenate([top, low, top, low], axis=0).T.astype(BF16)
+        hot_out[b * 256 : (b + 1) * 256, :] = hots[b * 384 + 128 : (b + 1) * 384, :]
+
+    def chunk(i, _):
+        lanes = pl.ds(pl.multiple_of(i * 128, 128), 128)
+        table = jnp.concatenate([tab_all[j, :, lanes] for j in range(3)], axis=1)
+        high = table.astype(BF16)
+        low = (table - high.astype(F32)).astype(BF16)
+        both = jnp.concatenate([high, low], axis=0)
+        filtered = jnp.dot(hots[...], both, preferred_element_type=F32)
+        gated = filtered[:, 128:256] * filtered[:, 256:384]
+        g16 = gated.astype(BF16)
+        window = jnp.concatenate(
+            [g16[b * 384 + s * 128 : b * 384 + s * 128 + 256] for b in range(2) for s in range(2)], axis=1
+        )
+        lane_group = (lax.broadcasted_iota(jnp.int32, window.shape, 1) % 128) // 16
+        taps = taps_all[pl.ds(pl.multiple_of(i * 8, 8), 8), :]
+        total = jnp.zeros((128, 512), F32)
+        for g in range(8):
+            base = jnp.broadcast_to(taps[g : g + 1, :], (128, 256))
+            toep = pltpu.roll(base, 0, 1, stride=1, stride_axis=0).astype(BF16)
+            masked = jnp.where(lane_group == g, window, jnp.zeros_like(window))
+            total = total + jnp.dot(toep, masked, preferred_element_type=F32)
+        skip = tab_all[0, 12:13, lanes]
+        for b in range(2):
+            for s in range(2):
+                at = b * 384 + 128 + s * 128
+                part = total[:, (2 * b + s) * 128 : (2 * b + s + 1) * 128]
+                mixed = filtered[at : at + 128, 0:128] * (part + skip * gated[at : at + 128])
+                mix_ref[b * 256 + s * 128 : b * 256 + (s + 1) * 128, lanes] = mixed.astype(BF16)
+        return 0
+
+    lax.fori_loop(0, 4, chunk, 0)
+    gh.z_step(4)
+    gh.z_step(5)
+    for n, k in enumerate(KIND_ORDER):
+        lax.fori_loop(4 + 2 * n, 6 + 2 * n, chunk, 0)
         for side in range(3):
             gh.plane_step(side, k)
     gh.finish()
-    for d in (1, 2, 3):
-        ref = ids_out.at[pl.ds(((y + 4 - d) % 4) * 16, 16)]
-        remote(ref, ref, s_ids.at[0], r_ids.at[5 + d], partners[0]).wait_recv()
-        ref = pack_out.at[(t + 4 - d) % 4]
-        remote(ref, ref, s_ids.at[0], r_pack.at[d - 1], partners[0]).wait_recv()
     for c in small:
         c.wait_send()
-    keep_pack.wait()
-
-
-def gather_all(ids, pack, wh, wa):
+
+
+def hyena(ids8, hit, emb4, gain, in_proj, short, taps, skip, wh):
     dma = pltpu.SemaphoreType.DMA
+    vmem = pl.BlockSpec(memory_space=pltpu.VMEM)
     return pl.pallas_call(
-        gather_kernel,
+        hyena_kernel,
         out_shape=(
-            jax.ShapeDtypeStruct((64, 1, 128), jnp.int32),
-            jax.ShapeDtypeStruct((4,) + pack.shape, F32),
+            jax.ShapeDtypeStruct((512, 2048), BF16),
+            jax.ShapeDtypeStruct((512, 32), BF16),
             jax.ShapeDtypeStruct((2048, 4096), BF16),
         ),
-        in_specs=[ANY] * 4,
-        out_specs=(ANY,) * 3,
+        in_specs=[vmem, pl.BlockSpec(memory_space=pltpu.SMEM), vmem, vmem, ANY, vmem, vmem, vmem, ANY],
+        out_specs=(vmem, vmem, ANY),
         scratch_shapes=[
-            dma((N_SENDS,)), dma((48,)), dma((N_SENDS,)), dma((48,)),
-            dma((9,)), dma((9,)), dma((3,)), dma((3,)),
-            pltpu.VMEM(wh.shape, BF16), pltpu.VMEM(wa.shape, BF16), dma((2,)), dma((2,)), dma((2,)),
+            pltpu.VMEM((64, 8, 128), jnp.int32),
+            pltpu.VMEM((3, 16, 2048), F32),
+            pltpu.VMEM((128, 256), F32),
+            pltpu.VMEM((768, 32), BF16),
+            pltpu.VMEM(in_proj.shape, BF16),
+            pltpu.VMEM(wh.shape, BF16),
+            dma((N_SENDS,)), dma((48,)), dma((2,)),
+            dma((9,)), dma((9,)), dma((3,)), dma((3,)), dma((3,)), dma((3,)), dma((3,)),
         ],
         compiler_params=pltpu.CompilerParams(
-            collective_id=0, has_side_effects=True, vmem_limit_bytes=32 * 2**20
+            collective_id=0, has_side_effects=True, vmem_limit_bytes=48 * 2**20
         ),
-        name="gather_all",
-    )(ids, pack, wh, wa)
-
-
-def mix_kernel(onehot_ref, tab_ref, taps_ref, skip_ref, out_ref):
-    table = jnp.concatenate([tab_ref[0], tab_ref[1], tab_ref[2]], axis=1)
-    high = table.astype(BF16)
-    low = (table - high.astype(F32)).astype(BF16)
-    both = jnp.concatenate([high, low], axis=0)
-    filtered = jnp.dot(onehot_ref[...], both, preferred_element_type=F32)
-    gated = filtered[:, 128:256] * filtered[:, 256:384]
-    g16 = gated.astype(BF16)
-    window = jnp.concatenate(
-        [g16[b * 384 + s * 128 : b * 384 + s * 128 + 256] for b in range(2) for s in range(2)], axis=1
-    )
-    lane_group = (lax.broadcasted_iota(jnp.int32, window.shape, 1) % 128) // 16
-    total = jnp.zeros((128, 512), F32)
-    for g in range(8):
-        base = jnp.broadcast_to(taps_ref[g : g + 1, :], (128, 256))
-        toep = pltpu.roll(base, 0, 1, stride=1, stride_axis=0).astype(BF16)
-        masked = jnp.where(lane_group == g, window, jnp.zeros_like(window))
-        total = total + jnp.dot(toep, masked, preferred_element_type=F32)
-    for b in range(2):
-        for s in range(2):
-            at = b * 384 + 128 + s * 128
-            part = total[:, (2 * b + s) * 128 : (2 * b + s + 1) * 128]
-            mixed = filtered[at : at + 128, 0:128] * (part + skip_ref[...] * gated[at : at + 128])
-            out_ref[b * 256 + s * 128 : b * 256 + (s + 1) * 128, :] = mixed.astype(BF16)
-
-
-def hyena_mix(onehot, tab, taps, skip):
-    return pl.pallas_call(
-        mix_kernel,
-        out_shape=jax.ShapeDtypeStruct((512, 2048), BF16),
-        grid=(16,),
-        in_specs=[
-            pl.BlockSpec((768, 32), lambda i: (0, 0)),
-            pl.BlockSpec((3, 16, 128), lambda i: (0, 0, i)),
-            pl.BlockSpec((8, 256), lambda i: (i, 0)),
-            pl.BlockSpec((1, 128), lambda i: (0, i)),
-        ],
-        out_specs=pl.BlockSpec((512, 128), lambda i: (0, i)),
-        compiler_params=pltpu.CompilerParams(vmem_limit_bytes=40 * 2**20),
-        name="hyena_mix",
-    )(onehot, tab, taps, skip)
+        name="hyena",
+    )(ids8, hit, emb4, gain, in_proj, short, taps, skip, wh)
 
 
 def proj_kernel(t_ref, mix_ref, wh_ref, code_ref, emb_ref, gain_ref, wq_ref, cos_ref, sin_ref,
@@ -323,8 +353,8 @@
             in_specs=[
                 whole(512, 2048),
                 pl.BlockSpec((2048, 512), whi),
-                whole(512, 16),
-                pl.BlockSpec((16, 512), whi),
+                whole(512, 32),
+                pl.BlockSpec((32, 512), whi),
                 pl.BlockSpec((1, 512), whi),
                 pl.BlockSpec((1, 4096, 256), wqi),
                 whole(512, 128),
@@ -434,73 +464,64 @@
     )(qkv)
 
 
-KEYS = 1024
-
-
-def attend_kernel(slot_ref, q_hbm, kv_hbm, o_hbm, q_s, k_s, v_s, o_s, sem, osem):
+def attend_kernel(slot_ref, q_ref, kv_ref, o_ref):
     b = slot_ref[32]
 
-    def load(p, _):
-        slot = slot_ref[p]
-        c, i = slot // 2, slot % 2
-        pltpu.make_async_copy(q_hbm.at[c, i], q_s.at[pl.ds(pl.multiple_of(p * 64, 64), 64)], sem.at[0, p]).start()
-        rows = pl.ds(pl.multiple_of(p * 256, 256), 256)
-        pltpu.make_async_copy(kv_hbm.at[c, 0, i], k_s.at[rows], sem.at[1, p]).start()
-        pltpu.make_async_copy(kv_hbm.at[c, 1, i], v_s.at[rows], sem.at[2, p]).start()
-        return 0
-
-    lax.fori_loop(0, 32, load, 0)
-
-    for j in range(8):
-        for p in range(4 * j, 4 * j + 4):
-            pltpu.make_async_copy(q_hbm.at[0, 0], q_s.at[pl.ds(p * 64, 64)], sem.at[0, p]).wait()
-            pltpu.make_async_copy(kv_hbm.at[0, 0, 0], k_s.at[pl.ds(p * 256, 256)], sem.at[1, p]).wait()
-            pltpu.make_async_copy(kv_hbm.at[0, 1, 0], v_s.at[pl.ds(p * 256, 256)], sem.at[2, p]).wait()
-        q = q_s[pl.ds(j * 256, 256), :]
-
-        def step(start, carry, masked):
-            top, tot, acc = carry
-            keys = k_s[pl.ds(start, KEYS), :]
-            scores = lax.dot_general(q, keys, (((1,), (1,)), ((), ())), preferred_element_type=F32)
+    def q_tile(tile):
+        parts = []
+        for p in range(4 * tile, 4 * tile + 4):
+            slot = slot_ref[p]
+            parts.append(q_ref[slot // 2, slot % 2])
+        return jnp.concatenate(parts, axis=0)
+
+    def step(queries, carries, block, masked):
+        slots = [slot_ref[block + n] for n in range(4)]
+        keys = [kv_ref[s // 2, 0, s % 2] for s in slots]
+        vals = [kv_ref[s // 2, 1, s % 2] for s in slots]
+        scores = [
+            [lax.dot_general(q, k, (((1,), (1,)), ((), ())), preferred_element_type=F32) for k in keys] for q in queries
+        ]
+        done = []
+        for (top, tot, acc), score in zip(carries, scores):
             if masked:
-                r = lax.broadcasted_iota(jnp.int32, scores.shape, 0)
-                col = lax.broadcasted_iota(jnp.int32, scores.shape, 1)
-                qpos = (r // 64) * 256 + b * 64 + r % 64
-                scores = jnp.where(col <= qpos, scores, NEG_FILL)
-            new = jnp.maximum(top, jnp.max(scores, axis=1, keepdims=True))
-            w = jnp.exp2(scores - new)
+                for n in range(4):
+                    r = lax.broadcasted_iota(jnp.int32, (256, 256), 0)
+                    col = lax.broadcasted_iota(jnp.int32, (256, 256), 1) + n * 256
+                    score[n] = jnp.where(col <= (r // 64) * 256 + b * 64 + r % 64, score[n], NEG_FILL)
+            most = functools.reduce(jnp.maximum, score)
+            new = jnp.maximum(top, jnp.max(most, axis=1, keepdims=True))
             shrink = jnp.exp2(top - new)
-            tot = tot * shrink + jnp.sum(w, axis=1, keepdims=True)
-            acc = acc * shrink + jnp.dot(w.astype(BF16), v_s[pl.ds(start, KEYS), :], preferred_element_type=F32)
-            return new, tot, acc
-
-        first = (jnp.full((256, 1), NEG_FILL, F32), jnp.zeros((256, 1), F32), jnp.zeros((256, 128), F32))
-        carry = step(j * KEYS, first, True)
+            weights = [jnp.exp2(s - new) for s in score]
+            tot = tot * shrink + jnp.sum(functools.reduce(jnp.add, weights), axis=1, keepdims=True)
+            for n, (w, v) in enumerate(zip(weights, vals)):
+                part = jnp.dot(w.astype(BF16), v, preferred_element_type=F32)
+                add = part if n == 0 else add + part
+            done.append((new, tot, acc * shrink + add))
+        return tuple(done)
+
+    start = (jnp.full((256, 1), NEG_FILL, F32), jnp.zeros((256, 1), F32), jnp.zeros((256, 128), F32))
+    for j in range(0, 8, 2):
+        q0, q1 = q_tile(j), q_tile(j + 1)
+        c0 = step([q0], [start], 4 * j, True)[0]
+        c1 = step([q1], [start], 4 * j + 4, True)[0]
+        c1 = step([q1], [c1], 4 * j, False)[0]
+        carries = (c0, c1)
         if j:
-            carry = lax.fori_loop(0, j, lambda kc, c: step(pl.multiple_of(kc * KEYS, KEYS), c, False), carry)
-        top, tot, acc = carry
-        o_s[pl.ds(j * 256, 256), :] = (acc / tot).astype(BF16)
-        for p in range(4 * j, 4 * j + 4):
-            pltpu.make_async_copy(o_s.at[pl.ds(p * 64, 64)], o_hbm.at[slot_ref[p]], osem.at[p]).start()
-    for p in range(32):
-        pltpu.make_async_copy(o_s.at[pl.ds(p * 64, 64)], o_hbm.at[0], osem.at[p]).wait()
+            carries = lax.fori_loop(0, j, lambda n, c: step([q0, q1], c, 4 * n, False), carries, unroll=2)
+        for tile in range(2):
+            _, tot, acc = carries[tile]
+            out = (acc / tot).astype(BF16)
+            for n in range(4):
+                o_ref[slot_ref[4 * (j + tile) + n]] = out[n * 64 : (n + 1) * 64]
 
 
 def attend(slots, q_all, kv_all):
-    dma = pltpu.SemaphoreType.DMA
+    vmem = pl.BlockSpec(memory_space=pltpu.VMEM)
     return pl.pallas_call(
         attend_kernel,
         out_shape=jax.ShapeDtypeStruct((32, 64, 128), BF16),
-        in_specs=[pl.BlockSpec(memory_space=pltpu.SMEM), ANY, ANY],
-        out_specs=ANY,
-        scratch_shapes=[
-            pltpu.VMEM((2048, 128), BF16),
-            pltpu.VMEM((8192, 128), BF16),
-            pltpu.VMEM((8192, 128), BF16),
-            pltpu.VMEM((2048, 128), BF16),
-            dma((3, 32)),
-            dma((32,)),
-        ],
+        in_specs=[pl.BlockSpec(memory_space=pltpu.SMEM), vmem, vmem],
+        out_specs=vmem,
         compiler_params=pltpu.CompilerParams(vmem_limit_bytes=48 * 2**20),
         name="attend",
     )(slots, q_all, kv_all)
@@ -595,43 +616,21 @@
          hyena_out, attn_gain, qkv_proj, attn_out):
     dp, y, x, t = coords()
     ctx = y * 4 + x
-    codes = jnp.array(CODES, jnp.int32)
-    emb4 = jnp.concatenate([embed[c : c + 1] for c in CODES] + [jnp.zeros((12, embed.shape[1]), BF16)], axis=0)
-    wide = emb4.astype(F32)
-    normed = (wide * lax.rsqrt(jnp.mean(wide * wide, axis=-1, keepdims=True) + EPS) * mix_gain).astype(BF16)
-    projected = jnp.einsum("rd,jdc->jrc", normed, in_proj, preferred_element_type=F32).astype(BF16)[:, :4]
-    table = short_filter[:, :, None, :] * projected.astype(F32)[:, None]
-    pack = jnp.concatenate(
-        [table.reshape(-1), long_filter.reshape(-1), conv_skip.reshape(-1)]
-    ).reshape(-1, 128)
-    ids_all, packs, wh = gather_all(ids.reshape(1, 1, 128), pack, hyena_out, attn_out)
-    wa = lax.all_gather(lax.dynamic_slice_in_dim(attn_out, (dp * 16 + ctx) * 16, 16, 0), ("tensor", "dp", "context"), axis=0, tiled=True)
-
-    packs = packs.reshape(4, -1)
-    n_tab = 36 * 512
-    tab = packs[:, :n_tab].reshape(4, 3, 12, 512).transpose(1, 2, 0, 3).reshape(3, 12, 2048)
-    tab = jnp.concatenate([tab, jnp.zeros((3, 4, 2048), F32)], axis=1)
-    lf = packs[:, n_tab : n_tab + 4096].reshape(128, 128)
-    skip = packs[:, n_tab + 4096 :].reshape(1, 2048)
-    taps = jnp.concatenate([jnp.zeros((128, 1), F32), lf[:, ::-1], jnp.zeros((128, 127), F32)], axis=1)
-
-    ids_blocks = ids_all.reshape(32, 256)
+    emb4 = jnp.concatenate([embed[c : c + 1] for c in CODES] + [jnp.zeros((28, embed.shape[1]), BF16)], axis=0)
+    taps = jnp.concatenate(
+        [jnp.zeros((32, 1), F32), long_filter[:, ::-1], jnp.zeros((32, 127), F32)], axis=1
+    )
     slot_ids = jnp.arange(32, dtype=jnp.int32)
     pair = 2 * ctx + jnp.arange(2, dtype=jnp.int32)
     owned = jnp.sum(jnp.where(slot_ids[None] == pair[:, None], block_order[None], 0), axis=1)
-    own_ids = lax.dynamic_slice_in_dim(ids_blocks, 2 * ctx, 2, 0)
-    hit = block_order[None, :] == owned[:, None] - 1
-    prev_ids = jnp.sum(jnp.where(hit[:, :, None], ids_blocks[None, :, 126:], 0), axis=1)
-    ext = jnp.concatenate([prev_ids, own_ids], axis=1)
-    hots = [
-        (ext[:, 2 - tap : 2 - tap + 384, None] == codes).astype(BF16) for tap in range(3)
-    ]
-    hot16 = jnp.concatenate(hots + [jnp.zeros((2, 384, 4), BF16)], axis=-1).reshape(768, 16)
-    hot32 = jnp.concatenate([hot16, hot16], axis=1)
-    code_hot = jnp.concatenate(
-        [(own_ids.reshape(512, 1) == codes).astype(BF16), jnp.zeros((512, 12), BF16)], axis=1
+    hit = (block_order[None, :] == owned[:, None] - 1).astype(jnp.int32).reshape(64)
+    ids8 = jnp.broadcast_to(ids.reshape(1, 128), (8, 128))
+    mix, code_hot, wh = hyena(
+        ids8, hit, emb4, mix_gain.reshape(1, -1), in_proj, short_filter, taps, conv_skip.reshape(1, -1), hyena_out
     )
-    mix = hyena_mix(hot32, tab, taps, skip)
+    wa = lax.all_gather(
+        lax.dynamic_slice_in_dim(attn_out, (dp * 16 + ctx) * 16, 16, 0), ("tensor", "dp", "context"), axis=0, tiled=True
+    )
 
     local_pos = (owned[:, None] * 256 + jnp.arange(256, dtype=jnp.int32)[None]).reshape(512)
     inverse_freq = THETA ** (-(2.0 * jnp.arange(64, dtype=F32)) / HD)

time: 229 us -> 189 us (0.83)
  Pallas kernels: 182 us -> 148 us
  matrix products: 16 us -> 9.52 us
    pallas_call x2 -> x1, Pallas kernels: 75.5 us -> 57.5 us  [hyena(): pl.pallas_call(hyena_kernel, out_shape=(jax.ShapeDtypeStruct((512, 2048),...]
    pallas_call x1, Pallas kernels: 34.1 us -> 16.6 us  [attend(): pl.pallas_call(attend_kernel, out_shape=jax.ShapeDtypeStruct((32, 64, 128...]
    dot_general x1 -> x0, matrix products: 6.51 us -> none  [body(): jnp.einsum('rd,jdc->jrc', normed, in_proj, preferred_element_type=F32)]
    unnamed x35 -> x21, local copies, waits for them, and re-layouts: 7.08 us -> 7.4 us
  transfers between devices with their start and end apart: 1 -> 1, of which waited for: 0 -> 0; matrix products, arithmetic and copies ran while one was open for 6% -> 4% of each run, Pallas kernels for 80% -> 79%
where the time goes in v3:
time: 189 us; the launch traced here: 188 us
  Pallas kernels  148 us (78%)
  local copies, waits for them, and re-layouts  13.5 us (7%)
  between operations  13.5 us (7%)
  matrix products  9.52 us (5%)
  other arithmetic  3.12 us (2%)
    pallas_call x1, Pallas kernels, hyena(): pl.pallas_call(hyena_kernel, out_shape=(jax.ShapeDtypeStruct((512, 2048),...  57.5 us
    pallas_call x1, Pallas kernels, exchange(): pl.pallas_call(exchange_kernel, out_shape=(jax.ShapeDtypeStruct((16, 2, 6...  33 us
    pallas_call x1, Pallas kernels, stream_qkv(): pl.pallas_call(proj_kernel, out_shape=(jax.ShapeDtypeStruct((128, 4096),...  25.8 us
    pallas_call x1, Pallas kernels, attend(): pl.pallas_call(attend_kernel, out_shape=jax.ShapeDtypeStruct((32, 64, 128...  16.6 us
    pallas_call x1, Pallas kernels, give_back(): pl.pallas_call(return_kernel, out_shape=jax.ShapeDtypeStruct((32, 64, 128...  15.4 us
    dot_general x1, matrix products, body(): return stream_own + jnp.dot(att, wa, preferred_element_type=F32)  9.52 us
    unnamed x21, local copies, waits for them, and re-layouts  7.4 us
  transfers between devices with their start and end apart: 1, of which 0 were waited for; matrix products, arithmetic and copies ran while one was open for 4% of the time, Pallas kernels for 79%

profile of v3, /device:TPU:1, one launch (start us, length us, event | category | flops | bytes accessed | tf_op | source)
XLA Modules:
  0.0 188.2 jit_solution(18198337110488857340)
XLA Ops:
  6.5 0.0 all-gather.2.cloned.1.call-start
  6.5 1.5 constant_dynamic-slice_fusion
  8.1 0.0 all-gather.2.cloned.1.call-update
  8.1 0.8 fusion.1
  9.0 0.7 compare_convert_fusion
  9.7 0.1 reshape.75.hit_ref
  9.8 0.8 rev.3
  10.6 0.1 pad.8.clone
  10.7 0.1 convert_bitcast_fusion
  10.7 1.1 fusion.2
  11.8 0.6 concatenate.15.emb_ref
  12.4 0.1 maximum_maximum_fusion.taps_ref
  12.5 0.7 broadcast_in_dim.26.ids_ref
  13.1 0.0 copy-start.5
  13.2 0.7 copy-done.5
  13.9 0.0 copy-start.7
  13.9 0.7 copy-done.7
  14.6 0.0 copy-start.8
  14.6 0.7 copy-done.8
  15.3 0.0 copy-start.6
  15.3 57.5 %hyena.1 = (bf16[512,2048]{1,0:T(8,128)(2,1)S(1)}, bf16[512,32]{1,0:T(8,128)(2,1)S(1)}, bf16[2048,4096]{1,0:T(8,128)(2,1)}) custom-call(s32[8,128]{1,0:T(8,128)S(1)} %broadcast_in_dim.26.ids_ref, s32[64]{0:T(128)S(1)} %reshape.75.hit_ref, bf16[32,4096]{1,0:T(8,128)(2,1)S(1)} %concatenate.15.emb_ref, f32[1,4096]{1,0:T(1,128)S(1)} %bitcast.18, ...), custom_call_target="tpu_custom_call" | custom-call | tf_op jit(solution)/shard_map/hyena/pallas_call | solution.py:272
  72.8 0.0 copy-start.1
  72.8 1.0 fusion
  73.8 0.2 pad_maximum_fusion
  74.0 0.1 copy-done.1
  74.1 0.0 copy-done.6
  74.1 0.0 copy-start.9
  74.1 25.8 %stream_qkv.1 = (f32[128,4096]{1,0:T(8,128)S(1)}, bf16[4,3,2,4,64,128]{5,4,3,2,1,0:T(8,128)(2,1)S(1)}) custom-call(s32[1]{0:T(128)} %bitcast.t_ref, bf16[512,2048]{1,0:T(8,128)(2,1)} %copy-done.1, bf16[2048,4096]{1,0:T(8,128)(2,1)} %get-tuple-element.13.wh_ref, bf16[512,32]{1,0:T(8,128)(2,1)S(1)} %get-tuple-element.14.code_ref, ...), custom_call_target="tpu_custom_call" | custom-call | tf_op jit(solution)/shard_map/stream_qkv/pallas_call | solution.py:344
  100.0 0.0 copy-start.3
  100.0 1.1 copy-done.3
  101.1 33.0 %exchange.1 = (bf16[16,2,64,128]{3,2,1,0:T(8,128)(2,1)}, bf16[16,2,2,4,64,128]{5,4,3,2,1,0:T(8,128)(2,1)}) custom-call(bf16[4,3,2,4,64,128]{5,4,3,2,1,0:T(8,128)(2,1)} %copy-done.3), custom_call_target="tpu_custom_call" | custom-call | tf_op jit(solution)/shard_map/exchange/pallas_call | solution.py:453
  134.2 0.0 copy-done.9
  134.2 0.1 select_reduce_fusion
  134.3 0.1 pad_add_fusion.slot_ref
  134.4 0.0 copy-start
  134.4 2.2 %copy-done = bf16[16,2,2,4,64,128]{5,4,3,2,1,0:T(8,128)(2,1)S(1)} copy-done((bf16[16,2,2,4,64,128]{5,4,3,2,1,0:T(8,128)(2,1)S(1)}, bf16[16,2,2,4,64,128]{5,4,3,2,1,0:T(8,128)(2,1)}, u32[]{:S(2)}) %copy-start) | copy-done | bytes 4194328
  136.6 0.0 copy-start.4
  136.6 1.0 copy-done.4
  137.6 16.6 %attend.1.o_ref = bf16[32,64,128]{2,1,0:T(8,128)(2,1)S(1)} custom-call(s32[33]{0:T(128)S(1)} %pad_add_fusion.slot_ref, bf16[16,2,64,128]{3,2,1,0:T(8,128)(2,1)S(1)} %copy-done.4, bf16[16,2,2,256,128]{4,3,2,1,0:T(8,128)(2,1)S(1)} %bitcast.16), custom_call_target="tpu_custom_call" | custom-call | tf_op jit(solution)/shard_map/attend/pallas_call | solution.py:520
  154.2 0.0 copy-start.2
  154.2 0.8 copy-done.2
  155.0 15.4 %give_back.1 = bf16[32,64,128]{2,1,0:T(8,128)(2,1)} custom-call(bf16[32,64,128]{2,1,0:T(8,128)(2,1)} %copy-done.2), custom_call_target="tpu_custom_call" | custom-call | tf_op jit(solution)/shard_map/give_back/pallas_call | solution.py:604
  170.4 1.3 copy.14
  171.8 0.0 all-gather.2.cloned.1.call-done
  171.8 9.5 %convolution_add_fusion = f32[128,4096]{1,0:T(8,128)} fusion(f32[128,4096]{1,0:T(8,128)S(1)} %get-tuple-element.15, bf16[128,2048]{0,1:T(8,128)(2,1)S(1)} %bitcast.20, bf16[2048,4096]{1,0:T(8,128)(2,1)} %all-gather.2.cloned.1.call-done), kind=kOutput, calls=%fused_computation | convolution fusion | flops 2148007936 | bytes 21495808 | tf_op jit(solution)/shard_map/dot_general | solution.py:651
  (7 shorter events, 0.1 us)
Async XLA Ops:
  6.5 165.2 %all-gather.2.cloned.1.call-start = ((), (), s32[]{:S(2)}) async-start(), calls=%async_computation | async-start | bytes 16908288 | tf_op jit(solution)/shard_map/all_gather | solution.py:631
  13.1 0.7 copy-start.5
  13.9 0.7 copy-start.7
  14.6 0.7 copy-start.8
  15.3 58.8 %copy-start.6 = (f32[4096]{0:T(1024)S(1)}, f32[4096]{0:T(1024)}, u32[]{:S(2)}) copy-start(f32[4096]{0:T(1024)} %param.21) | copy-start | bytes 49156
  72.8 1.3 copy-start.1
  74.1 60.0 %copy-start.9 = (s32[32]{0:T(128)S(1)}, s32[32]{0:T(128)}, u32[]{:S(2)}) copy-start(s32[32]{0:T(128)} %param.13) | copy-start | bytes 388
  100.0 1.1 copy-start.3
  134.4 2.2 %copy-start = (bf16[16,2,2,4,64,128]{5,4,3,2,1,0:T(8,128)(2,1)S(1)}, bf16[16,2,2,4,64,128]{5,4,3,2,1,0:T(8,128)(2,1)}, u32[]{:S(2)}) copy-start(bf16[16,2,2,4,64,128]{5,4,3,2,1,0:T(8,128)(2,1)} %get-tuple-element.18) | copy-start | bytes 12582916
  136.6 1.0 copy-start.4
  154.2 0.8 copy-start.2
Sparse Core Ops, SparseCore 0:
  10.5 86.7 all-gather.1

commit v4 on v3

--- a/solution.py
+++ b/solution.py
@@ -295,9 +295,31 @@
     )(ids8, hit, emb4, gain, in_proj, short, taps, skip, wh)
 
 
-def proj_kernel(t_ref, mix_ref, wh_ref, code_ref, emb_ref, gain_ref, wq_ref, cos_ref, sin_ref,
-                own_ref, qkv_ref, attn_in, chunk, squares):
+def ab_of(dp, y, x):
+    return pick(dp, y, x), pick(dp, x, y)
+
+
+def ctx_of(dp, a, b):
+    return pick(dp, a * 4 + b, b * 4 + a)
+
+
+ORDER = (1, 3, 2)
+
+
+def proj_kernel(mix_ref, wh_ref, code_ref, emb_ref, gain_ref, wq_ref, cos_ref, sin_ref,
+                own_ref, q_out, kv_out, attn_in, chunk, squares, qkv, s1, r1, s2, r2, s3, r3, sq, rq, loc):
     i = pl.program_id(0)
+    dp, y, x, t = coords()
+    ctx = y * 4 + x
+    a, b = ab_of(dp, y, x)
+    others = [{"context": (ctx + d) % 16} for d in range(1, 16)]
+    barrier = pltpu.get_barrier_semaphore()
+
+    @pl.when(i == 0)
+    def _():
+        squares[...] = jnp.zeros_like(squares)
+        for where in others:
+            pl.semaphore_signal(barrier, inc=1, device_id=where, device_id_type=MESH_ID)
 
     @pl.when(i < 8)
     def _():
@@ -305,19 +327,14 @@
         vals = vals + jnp.dot(code_ref[...], emb_ref[...], preferred_element_type=F32)
         chunk[...] = vals
         part = jnp.sum(vals * vals, axis=1, keepdims=True)
-
-        @pl.when(i == 0)
-        def _():
-            squares[...] = jnp.zeros_like(squares)
-
         squares[...] += jnp.broadcast_to(part, squares.shape)
         attn_in[:, pl.ds(pl.multiple_of(i * 512, 512), 512)] = (vals * gain_ref[...]).astype(BF16)
-        own_ref[...] = chunk[pl.ds(pl.multiple_of(t_ref[0] * 128, 128), 128), :]
+        own_ref[...] = chunk[pl.ds(pl.multiple_of(t * 128, 128), 128), :]
 
     @pl.when(i >= 8)
     def _():
         k = i - 8
-        j = k // 2
+        j = (k // 2 + 1) % 3
         factor = lax.rsqrt(squares[...] / 4096.0 + EPS)
         factor = factor * jnp.where(j == 0, HD**-0.5 * math.log2(math.e), 1.0).astype(F32)
         rotated = j < 2
@@ -327,141 +344,140 @@
         for hh in range(2):
             head = vals[:, hh * 128 : (hh + 1) * 128]
             turned = head * cos + pltpu.roll(head, 64, 1) * sin
-            qkv_ref[2 * (k % 2) + hh, j] = turned.astype(BF16).reshape(2, 4, 64, 128)
-
-
-def stream_qkv(t_arr, mix, wh, code_hot, emb4, gain, wq, cos, sin):
-    def whi(i, t):
+            qkv[2 * (k % 2) + hh, j] = turned.astype(BF16).reshape(2, 4, 64, 128)
+
+    bp = {"context": ctx_of(dp, a, (b + 1) % 4)}
+    bm = {"context": ctx_of(dp, a, (b + 3) % 4)}
+
+    def held(part, k, off):
+        return kv_out.at[ctx_of(dp, (a + 4 - k) % 4, (b + off) % 4), part]
+
+    def to_head(part, d):
+        h = (a + d) % 4
+        return remote(qkv.at[h, 1 + part], kv_out.at[ctx, part], s1.at[3 * part + d - 1], r1.at[3 * part + d - 1],
+                      {"context": ctx_of(dp, h, b)})
+
+    def spread(part, side, k):
+        src = qkv.at[a, 1 + part] if k == 0 else held(part, k, 0)
+        at = 8 * part + 4 * side + k
+        return remote(src, held(part, k, 0), s2.at[at], r2.at[at], (bp, bm)[side])
+
+    def relay(part, k):
+        ref = held(part, k, (3, 1)[part])
+        return remote(ref, ref, s3.at[4 * part + k], r3.at[4 * part + k], (bp, bm)[part])
+
+    def query(d):
+        to = (ctx + d) % 16
+        h, s = ab_of(dp, to // 4, to % 4)
+        return remote(qkv.at[h, 0, :, s], q_out.at[ctx], sq.at[d - 1], rq.at[d - 1], others[d - 1])
+
+    def landed(ref, recv):
+        remote(ref, ref, s1.at[0], recv, bp).wait_recv()
+
+    keeps = [
+        pltpu.make_async_copy(qkv.at[a, 1], kv_out.at[ctx, 0], loc.at[0]),
+        pltpu.make_async_copy(qkv.at[a, 2], kv_out.at[ctx, 1], loc.at[1]),
+        pltpu.make_async_copy(qkv.at[a, 0, :, b], q_out.at[ctx], loc.at[2]),
+    ]
+
+    def leave(part):
+        for d in ORDER:
+            to_head(part, d).start()
+        for side in range(2):
+            spread(part, side, 0).start()
+        keeps[part].start()
+
+    def pass_on(part):
+        for d in ORDER:
+            landed(held(part, d, 0), r1.at[3 * part + d - 1])
+            for side in range(2):
+                spread(part, side, d).start()
+
+    @pl.when(i == 9)
+    def _():
+        pl.semaphore_wait(barrier, 15)
+        leave(0)
+
+    @pl.when(i == 11)
+    def _():
+        leave(1)
+        pass_on(0)
+
+    @pl.when(i == 13)
+    def _():
+        pass_on(1)
+        keeps[2].start()
+        for d in range(1, 16):
+            query(d).start()
+        for part in range(2):
+            for k in (0,) + ORDER:
+                landed(held(part, k, (3, 1)[part]), r2.at[8 * part + 4 * part + k])
+                relay(part, k).start()
+        for part in range(2):
+            for k in (0,) + ORDER:
+                landed(held(part, k, (1, 3)[part]), r2.at[8 * part + 4 * (1 - part) + k])
+        for d in range(1, 16):
+            landed(q_out.at[(ctx + 16 - d) % 16], rq.at[d - 1])
+        for part in range(2):
+            for k in (0,) + ORDER:
+                landed(held(part, k, 2), r3.at[4 * part + k])
+        for part in range(2):
+            for d in ORDER:
+                to_head(part, d).wait_send()
+            for k in range(4):
+                for side in range(2):
+                    spread(part, side, k).wait_send()
+                relay(part, k).wait_send()
+        for d in range(1, 16):
+            query(d).wait_send()
+        for c in keeps:
+            c.wait()
+
+
+def stream_qkv(mix, wh, code_hot, emb4, gain, wq, cos, sin):
+    dma = pltpu.SemaphoreType.DMA
+
+    def whi(i):
         return (0, jnp.minimum(i, 7))
 
-    def wqi(i, t):
+    def wqi(i):
         k = jnp.maximum(i - 8, 0)
-        return (k // 2, 0, k % 2)
+        return ((k // 2 + 1) % 3, 0, k % 2)
 
     def whole(*shape):
-        return pl.BlockSpec(shape, lambda i, t: (0,) * len(shape))
+        return pl.BlockSpec(shape, lambda i: (0,) * len(shape))
 
     return pl.pallas_call(
         proj_kernel,
         out_shape=(
             jax.ShapeDtypeStruct((128, 4096), F32),
-            jax.ShapeDtypeStruct((4, 3, 2, 4, 64, 128), BF16),
-        ),
-        grid_spec=pltpu.PrefetchScalarGridSpec(
-            num_scalar_prefetch=1,
-            grid=(14,),
-            in_specs=[
-                whole(512, 2048),
-                pl.BlockSpec((2048, 512), whi),
-                whole(512, 32),
-                pl.BlockSpec((32, 512), whi),
-                pl.BlockSpec((1, 512), whi),
-                pl.BlockSpec((1, 4096, 256), wqi),
-                whole(512, 128),
-                whole(512, 128),
-            ],
-            out_specs=(
-                pl.BlockSpec((128, 512), whi),
-                whole(4, 3, 2, 4, 64, 128),
-            ),
-            scratch_shapes=[
-                pltpu.VMEM((512, 4096), BF16),
-                pltpu.VMEM((512, 512), F32),
-                pltpu.VMEM((512, 128), F32),
-            ],
-        ),
-        compiler_params=pltpu.CompilerParams(vmem_limit_bytes=48 * 2**20),
-        name="stream_qkv",
-    )(t_arr, mix, wh, code_hot, emb4, gain, wq, cos, sin)
-
-
-def ab_of(dp, y, x):
-    return pick(dp, y, x), pick(dp, x, y)
-
-
-def ctx_of(dp, a, b):
-    return pick(dp, a * 4 + b, b * 4 + a)
-
-
-def exchange_kernel(qkv_ref, q_out, kv_out, sq, rq, s1, r1, s2, r2, s3, r3, loc):
-    dp, y, x, t = coords()
-    ctx = y * 4 + x
-    a, b = ab_of(dp, y, x)
-    barrier = pltpu.get_barrier_semaphore()
-    others = [{"context": (ctx + d) % 16} for d in range(1, 16)]
-    for where in others:
-        pl.semaphore_signal(barrier, inc=1, device_id=where, device_id_type=MESH_ID)
-    pl.semaphore_wait(barrier, 15)
-    sent = []
-    keep_kv = pltpu.make_async_copy(qkv_ref.at[a, pl.ds(1, 2)], kv_out.at[ctx], loc.at[0])
-    keep_kv.start()
-    bp = {"context": ctx_of(dp, a, (b + 1) % 4)}
-    bm = {"context": ctx_of(dp, a, (b + 3) % 4)}
-
-    def spread(src, k, src_ctx):
-        for side, where in ((0, bp), (1, bm)):
-            c = remote(src, kv_out.at[src_ctx], s2.at[side * 4 + k], r2.at[side * 4 + k], where)
-            c.start()
-            sent.append(c)
-
-    for d in (1, 3, 2):
-        h = (a + d) % 4
-        c = remote(qkv_ref.at[h, pl.ds(1, 2)], kv_out.at[ctx], s1.at[d - 1], r1.at[d - 1], {"context": ctx_of(dp, h, b)})
-        c.start()
-        sent.append(c)
-    spread(qkv_ref.at[a, pl.ds(1, 2)], 0, ctx)
-    for d in range(1, 16):
-        to = (ctx + d) % 16
-        h, s = ab_of(dp, to // 4, to % 4)
-        c = remote(qkv_ref.at[h, 0, :, s], q_out.at[ctx], sq.at[d - 1], rq.at[d - 1], others[d - 1])
-        c.start()
-        sent.append(c)
-    keep_q = pltpu.make_async_copy(qkv_ref.at[a, 0, :, b], q_out.at[ctx], loc.at[1])
-    keep_q.start()
-    for d in (1, 3, 2):
-        from_ctx = ctx_of(dp, (a + 4 - d) % 4, b)
-        ref = kv_out.at[from_ctx]
-        remote(ref, ref, s1.at[0], r1.at[d - 1], bp).wait_recv()
-        spread(ref, d, from_ctx)
-    for k in (0, 1, 3, 2):
-        ua = (a + 4 - k) % 4
-        ref = kv_out.at[ctx_of(dp, ua, (b + 3) % 4)]
-        remote(ref, ref, s1.at[0], r2.at[k], bp).wait_recv()
-        c = remote(ref.at[0], ref.at[0], s3.at[k], r3.at[k], bp)
-        c.start()
-        sent.append(c)
-        ref = kv_out.at[ctx_of(dp, ua, (b + 1) % 4)]
-        remote(ref, ref, s1.at[0], r2.at[4 + k], bp).wait_recv()
-        c = remote(ref.at[1], ref.at[1], s3.at[4 + k], r3.at[4 + k], bm)
-        c.start()
-        sent.append(c)
-    for k in (0, 1, 3, 2):
-        ref = kv_out.at[ctx_of(dp, (a + 4 - k) % 4, (b + 2) % 4)]
-        for part in (0, 1):
-            remote(ref.at[part], ref.at[part], s1.at[0], r3.at[4 * part + k], bp).wait_recv()
-    for d in range(1, 16):
-        ref = q_out.at[(ctx + 16 - d) % 16]
-        remote(ref, ref, s1.at[0], rq.at[d - 1], bp).wait_recv()
-    for c in sent:
-        c.wait_send()
-    keep_q.wait()
-    keep_kv.wait()
-
-
-def exchange(qkv):
-    dma = pltpu.SemaphoreType.DMA
-    return pl.pallas_call(
-        exchange_kernel,
-        out_shape=(
             jax.ShapeDtypeStruct((16, 2, 64, 128), BF16),
             jax.ShapeDtypeStruct((16, 2, 2, 4, 64, 128), BF16),
         ),
-        in_specs=[ANY],
-        out_specs=(ANY,) * 2,
-        scratch_shapes=[dma((15,)), dma((15,)), dma((3,)), dma((3,)), dma((8,)), dma((8,)), dma((8,)), dma((8,)), dma((2,))],
-        compiler_params=pltpu.CompilerParams(collective_id=1, has_side_effects=True),
-        name="exchange",
-    )(qkv)
+        grid=(14,),
+        in_specs=[
+            whole(512, 2048),
+            pl.BlockSpec((2048, 512), whi),
+            whole(512, 32),
+            pl.BlockSpec((32, 512), whi),
+            pl.BlockSpec((1, 512), whi),
+            pl.BlockSpec((1, 4096, 256), wqi),
+            whole(512, 128),
+            whole(512, 128),
+        ],
+        out_specs=(pl.BlockSpec((128, 512), whi), ANY, ANY),
+        scratch_shapes=[
+            pltpu.VMEM((512, 4096), BF16),
+            pltpu.VMEM((512, 512), F32),
+            pltpu.VMEM((512, 128), F32),
+            pltpu.VMEM((4, 3, 2, 4, 64, 128), BF16),
+            dma((6,)), dma((6,)), dma((16,)), dma((16,)), dma((8,)), dma((8,)), dma((15,)), dma((15,)), dma((3,)),
+        ],
+        compiler_params=pltpu.CompilerParams(
+            collective_id=1, has_side_effects=True, vmem_limit_bytes=48 * 2**20
+        ),
+        name="stream_qkv",
+    )(mix, wh, code_hot, emb4, gain, wq, cos, sin)
 
 
 def attend_kernel(slot_ref, q_ref, kv_ref, o_ref):
@@ -512,22 +528,10 @@
             _, tot, acc = carries[tile]
             out = (acc / tot).astype(BF16)
             for n in range(4):
-                o_ref[slot_ref[4 * (j + tile) + n]] = out[n * 64 : (n + 1) * 64]
-
-
-def attend(slots, q_all, kv_all):
-    vmem = pl.BlockSpec(memory_space=pltpu.VMEM)
-    return pl.pallas_call(
-        attend_kernel,
-        out_shape=jax.ShapeDtypeStruct((32, 64, 128), BF16),
-        in_specs=[pl.BlockSpec(memory_space=pltpu.SMEM), vmem, vmem],
-        out_specs=vmem,
-        compiler_params=pltpu.CompilerParams(vmem_limit_bytes=48 * 2**20),
-        name="attend",
-    )(slots, q_all, kv_all)
-
-
-def return_kernel(o_ref, att_out, send, recv, loc):
+                o_ref[4 * (j + tile) + n] = out[n * 64 : (n + 1) * 64]
+
+
+def attend_return_kernel(slot_ref, q_ref, kv_ref, att_out, o_pos, o_ref, send, recv, loc):
     dp, y, x, t = coords()
     ctx = y * 4 + x
     a, b = ab_of(dp, y, x)
@@ -550,6 +554,9 @@
         return 0
 
     lax.fori_loop(0, 32, hello, 0)
+    attend_kernel(slot_ref, q_ref, kv_ref, o_pos)
+    for slot in range(32):
+        o_ref[slot] = o_pos[slot_ref[33 + slot]]
     has_self = (b // 2 == t % 2).astype(jnp.int32)
     pl.semaphore_wait(barrier, 32 - has_self)
     mine = (t * 4 + a) * 2 + b % 2
@@ -599,17 +606,22 @@
     lax.fori_loop(0, 32, finish, 0)
 
 
-def give_back(o):
+def attend_return(slots, q_all, kv_all):
     dma = pltpu.SemaphoreType.DMA
+    vmem = pl.BlockSpec(memory_space=pltpu.VMEM)
     return pl.pallas_call(
-        return_kernel,
+        attend_return_kernel,
         out_shape=jax.ShapeDtypeStruct((32, 64, 128), BF16),
-        in_specs=[ANY],
+        in_specs=[pl.BlockSpec(memory_space=pltpu.SMEM), vmem, vmem],
         out_specs=ANY,
-        scratch_shapes=[dma((32,)), dma((32,)), dma],
-        compiler_params=pltpu.CompilerParams(collective_id=2, has_side_effects=True),
-        name="give_back",
-    )(o)
+        scratch_shapes=[
+            pltpu.VMEM((32, 64, 128), BF16), pltpu.VMEM((32, 64, 128), BF16), dma((32,)), dma((32,)), dma
+        ],
+        compiler_params=pltpu.CompilerParams(
+            collective_id=2, has_side_effects=True, vmem_limit_bytes=48 * 2**20
+        ),
+        name="attend_return",
+    )(slots, q_all, kv_all)
 
 
 def body(ids, block_order, embed, mix_gain, in_proj, short_filter, long_filter, conv_skip,
@@ -638,15 +650,13 @@
     cos, sin = jnp.cos(angles), jnp.sin(angles)
     cos = jnp.concatenate([cos, cos], axis=1)
     sin = jnp.concatenate([-sin, sin], axis=1)
-    stream_own, qkv = stream_qkv(
-        t.astype(jnp.int32).reshape(1), mix, wh, code_hot, emb4, attn_gain.reshape(1, -1), qkv_proj, cos, sin
+    stream_own, q_all, kv_all = stream_qkv(
+        mix, wh, code_hot, emb4, attn_gain.reshape(1, -1), qkv_proj, cos, sin
     )
-    q_all, kv_all = exchange(qkv)
     slot_of = jnp.sum(jnp.where(block_order[None, :] == slot_ids[:, None], slot_ids[None, :], 0), axis=1)
     _, b = ab_of(dp, y, x)
-    slots = jnp.concatenate([slot_of, b.astype(jnp.int32).reshape(1)])
-    att = attend(slots, q_all, kv_all.reshape(16, 2, 2, 256, 128))
-    att = give_back(att)
+    slots = jnp.concatenate([slot_of, b.astype(jnp.int32).reshape(1), block_order])
+    att = attend_return(slots, q_all, kv_all.reshape(16, 2, 2, 256, 128))
     att = att.reshape(16, 128, 128).transpose(1, 0, 2).reshape(128, 2048)
     return stream_own + jnp.dot(att, wa, preferred_element_type=F32)
 

time: 189 us -> 174 us (0.921)
  Pallas kernels: 148 us -> 137 us
  local copies, waits for them, and re-layouts: 13.5 us -> 9.52 us
    pallas_call x3 -> x1, Pallas kernels: 65.1 us -> 29.6 us  [attend_return(): pl.pallas_call(attend_return_kernel, out_shape=jax.ShapeDtypeStruct((32,...]
    pallas_call x1, Pallas kernels: 25.8 us -> 50 us  [stream_qkv(): pl.pallas_call(proj_kernel, out_shape=(jax.ShapeDtypeStruct((128, 4096),...]
    unnamed x21 -> x13, local copies, waits for them, and re-layouts: 7.4 us -> 4.35 us
where the time goes in v4:
time: 174 us; the launch traced here: 173 us
  Pallas kernels  137 us (79%)
  between operations  13.5 us (8%)
  matrix products  9.53 us (5%)
  local copies, waits for them, and re-layouts  9.52 us (5%)
  other arithmetic  3.12 us (2%)
    pallas_call x1, Pallas kernels, hyena(): pl.pallas_call(hyena_kernel, out_shape=(jax.ShapeDtypeStruct((512, 2048),...  57.5 us
    pallas_call x1, Pallas kernels, stream_qkv(): pl.pallas_call(proj_kernel, out_shape=(jax.ShapeDtypeStruct((128, 4096),...  50 us
    pallas_call x1, Pallas kernels, attend_return(): pl.pallas_call(attend_return_kernel, out_shape=jax.ShapeDtypeStruct((32,...  29.6 us
    dot_general x1, matrix products, body(): return stream_own + jnp.dot(att, wa, preferred_element_type=F32)  9.53 us
    unnamed x13, local copies, waits for them, and re-layouts  4.35 us
  transfers between devices with their start and end apart: 1, of which 0 were waited for; matrix products, arithmetic and copies ran while one was open for 4% of the time, Pallas kernels for 79%

profile of v4, /device:TPU:1, one launch (start us, length us, event | category | flops | bytes accessed | tf_op | source)
XLA Modules:
  0.0 172.9 jit_solution(5268860756722660799)
XLA Ops:
  6.5 0.0 all-gather.2.cloned.1.call-start
  6.5 1.6 constant_dynamic-slice_fusion
  8.1 0.0 all-gather.2.cloned.1.call-update
  8.1 0.8 fusion.1
  9.0 0.7 compare_convert_fusion
  9.7 0.1 reshape.71.hit_ref
  9.8 0.8 rev.3
  10.6 0.1 pad.9.clone
  10.7 0.1 convert_bitcast_fusion
  10.8 1.1 fusion.2
  11.8 0.6 concatenate.15.emb_ref
  12.4 0.1 maximum_maximum_fusion.taps_ref
  12.5 0.7 broadcast_in_dim.26.ids_ref
  13.2 0.0 copy-start.1
  13.2 0.7 copy-done.1
  13.9 0.0 copy-start.3
  13.9 0.7 copy-done.3
  14.6 0.0 copy-start.4
  14.6 0.7 copy-done.4
  15.3 0.0 copy-start.2
  15.3 57.5 %hyena.1 = (bf16[512,2048]{1,0:T(8,128)(2,1)S(1)}, bf16[512,32]{1,0:T(8,128)(2,1)S(1)}, bf16[2048,4096]{1,0:T(8,128)(2,1)}) custom-call(s32[8,128]{1,0:T(8,128)S(1)} %broadcast_in_dim.26.ids_ref, s32[64]{0:T(128)S(1)} %reshape.71.hit_ref, bf16[32,4096]{1,0:T(8,128)(2,1)S(1)} %concatenate.15.emb_ref, f32[1,4096]{1,0:T(1,128)S(1)} %bitcast.18, ...), custom_call_target="tpu_custom_call" | custom-call | tf_op jit(solution)/shard_map/hyena/pallas_call | solution.py:272
  72.8 1.0 fusion
  73.8 0.2 pad_maximum_fusion
  74.0 0.0 copy-done.2
  74.1 0.0 copy-start.5
  74.1 50.0 %stream_qkv.1 = (f32[128,4096]{1,0:T(8,128)S(1)}, bf16[16,2,64,128]{3,2,1,0:T(8,128)(2,1)S(1)}, bf16[16,2,2,4,64,128]{5,4,3,2,1,0:T(8,128)(2,1)}) custom-call(bf16[512,2048]{1,0:T(8,128)(2,1)S(1)} %get-tuple-element.11.mix_ref, bf16[2048,4096]{1,0:T(8,128)(2,1)} %get-tuple-element.12.wh_ref, bf16[512,32]{1,0:T(8,128)(2,1)S(1)} %get-tuple-element.13.code_ref, ...), custom_call_target="tpu_custom_call" | custom-call | tf_op jit(solution)/shard_map/stream_qkv/pallas_call | solution.py:450
  124.1 0.0 copy-done.5
  124.1 0.1 select_reduce_fusion
  124.2 0.1 pad_add_fusion.slot_ref
  124.3 0.0 copy-start
  124.3 2.2 %copy-done = bf16[16,2,2,4,64,128]{5,4,3,2,1,0:T(8,128)(2,1)S(1)} copy-done((bf16[16,2,2,4,64,128]{5,4,3,2,1,0:T(8,128)(2,1)S(1)}, bf16[16,2,2,4,64,128]{5,4,3,2,1,0:T(8,128)(2,1)}, u32[]{:S(2)}) %copy-start) | copy-done | bytes 4194328
  126.5 29.6 %attend_return.1 = bf16[32,64,128]{2,1,0:T(8,128)(2,1)S(1)} custom-call(s32[65]{0:T(128)S(1)} %pad_add_fusion.slot_ref, bf16[16,2,64,128]{3,2,1,0:T(8,128)(2,1)S(1)} %get-tuple-element.15.q_ref, bf16[16,2,2,256,128]{4,3,2,1,0:T(8,128)(2,1)S(1)} %bitcast.15), custom_call_target="tpu_custom_call" | custom-call | tf_op jit(solution)/shard_map/attend_return/pallas_call | solution.py:612
  156.1 0.3 copy.14
  156.5 0.0 all-gather.2.cloned.1.call-done
  156.5 9.5 %convolution_add_fusion = f32[128,4096]{1,0:T(8,128)} fusion(f32[128,4096]{1,0:T(8,128)S(1)} %get-tuple-element.14, bf16[128,2048]{0,1:T(8,128)(2,1)S(1)} %bitcast.20, bf16[2048,4096]{1,0:T(8,128)(2,1)} %all-gather.2.cloned.1.call-done), kind=kOutput, calls=%fused_computation | convolution fusion | flops 2148007936 | bytes 21495808 | tf_op jit(solution)/shard_map/dot_general | solution.py:661
  (7 shorter events, 0.1 us)
Async XLA Ops:
  6.5 149.9 %all-gather.2.cloned.1.call-start = ((), (), s32[]{:S(2)}) async-start(), calls=%async_computation | async-start | bytes 16908288 | tf_op jit(solution)/shard_map/all_gather | solution.py:643
  13.2 0.7 copy-start.1
  13.9 0.7 copy-start.3
  14.6 0.7 copy-start.4
  15.3 58.7 %copy-start.2 = (f32[4096]{0:T(1024)S(1)}, f32[4096]{0:T(1024)}, u32[]{:S(2)}) copy-start(f32[4096]{0:T(1024)} %param.21) | copy-start | bytes 49156
  74.1 50.1 %copy-start.5 = (s32[32]{0:T(128)S(1)}, s32[32]{0:T(128)}, u32[]{:S(2)}) copy-start(s32[32]{0:T(128)} %param.13) | copy-start | bytes 388
  124.3 2.2 %copy-start = (bf16[16,2,2,4,64,128]{5,4,3,2,1,0:T(8,128)(2,1)S(1)}, bf16[16,2,2,4,64,128]{5,4,3,2,1,0:T(8,128)(2,1)}, u32[]{:S(2)}) copy-start(bf16[16,2,2,4,64,128]{5,4,3,2,1,0:T(8,128)(2,1)} %get-tuple-element.16) | copy-start | bytes 12582916
Sparse Core Ops, SparseCore 0:
  10.5 87.1 all-gather.1

commit v5 on v4

--- a/solution.py
+++ b/solution.py
@@ -140,14 +140,19 @@
     return jnp.where(k < 2, jnp.where(k == 0, CODES[0], CODES[1]), jnp.where(k == 2, CODES[2], CODES[3]))
 
 
-def hyena_kernel(ids_ref, hit_ref, emb_ref, gain_ref, proj_ref, short_ref, taps_ref, skip_ref, wh_ref,
+def hyena_kernel(ids_ref, order_ref, emb_ref, gain_hbm, proj_ref, short_hbm, taps_ref, skip_hbm, wh_ref,
                  mix_ref, hot_out, wh_out,
-                 ids_all, tab_all, taps_all, hots, proj_s, hold,
-                 s_w, r_w, loc_w, s_ids, r_ids, s_tab, r_tab, s_taps, r_taps, p_sem):
+                 gain_ref, short_ref, skip_ref, ids_all, tab_all, taps_all, hots, proj_s, hold,
+                 s_w, r_w, loc_w, s_ids, r_ids, s_tab, r_tab, s_taps, r_taps, p_sem, a_sem):
     dp, y, x, t = coords()
     ctx = y * 4 + x
     loads = [pltpu.make_async_copy(proj_ref.at[j], proj_s.at[j], p_sem.at[j]) for j in range(3)]
-    for c in loads:
+    small_loads = [
+        pltpu.make_async_copy(gain_hbm, gain_ref, a_sem.at[0]),
+        pltpu.make_async_copy(short_hbm, short_ref, a_sem.at[1]),
+        pltpu.make_async_copy(skip_hbm, skip_ref, a_sem.at[2]),
+    ]
+    for c in small_loads + loads:
         c.start()
     barrier = pltpu.get_barrier_semaphore()
     zs = [{"tensor": (t + d) % 4} for d in (1, 2, 3)]
@@ -157,7 +162,7 @@
     for where in partners:
         pl.semaphore_signal(barrier, inc=1, device_id=where, device_id_type=MESH_ID)
     mine = ctx * 4 + t
-    ids_all[mine] = ids_ref[...]
+    ids_all[mine] = jnp.broadcast_to(ids_ref[...], (8, 128))
     trow = pl.ds(pl.multiple_of(t * 32, 32), 32)
     taps_all[trow, :] = taps_ref[...]
     pl.semaphore_wait(barrier, len(partners))
@@ -179,13 +184,16 @@
     for d in (0, 1, 2):
         go(taps_all.at[trow, :], s_taps.at[d], r_taps.at[d], zs[d])
 
+    for c in small_loads:
+        c.wait()
     wide = emb_ref[...].astype(F32)
     square = jnp.sum(wide * wide, axis=1, keepdims=True)
     normed = (wide * lax.rsqrt(square / 4096.0 + EPS) * gain_ref[...]).astype(BF16)
     cols = pl.ds(pl.multiple_of(t * 512, 512), 512)
     for j in range(3):
         loads[j].wait()
-        rows = jnp.dot(normed, proj_s[j], preferred_element_type=F32).astype(BF16).astype(F32)[0:4]
+        rows = jnp.dot(normed, proj_s[j], preferred_element_type=F32).astype(BF16).astype(F32)
+        rows = jnp.concatenate([rows[c - 64 : c - 63] for c in CODES], axis=0)
         last = jnp.broadcast_to(skip_ref[...], (4, 512))
         tab_all[j, :, cols] = jnp.concatenate([short_ref[j, tap : tap + 1, :] * rows for tap in range(3)] + [last], axis=0)
     for d in (0, 1, 2):
@@ -214,7 +222,7 @@
     for b in range(2):
         prev = [jnp.zeros((8, 128), jnp.int32) for _ in range(2)]
         for slot in range(32):
-            hit = hit_ref[b * 32 + slot]
+            hit = (order_ref[slot] == order_ref[2 * ctx + b] - 1).astype(jnp.int32)
             for half in range(2):
                 prev[half] = prev[half] + hit * ids_all[2 * slot + half]
         own = [ids_all[ctx * 4 + 2 * b + half] for half in range(2)]
@@ -223,7 +231,9 @@
         top = jnp.where(jnp.where(row8 < 4, back[0], back[1]) == code8, 1.0, 0.0)
         low = jnp.where(row8 < 4, jnp.where(back[2] == code8, 1.0, 0.0), 0.0)
         hots[b * 384 : (b + 1) * 384, :] = jnp.concatenate([top, low, top, low], axis=0).T.astype(BF16)
-        hot_out[b * 256 : (b + 1) * 256, :] = hots[b * 384 + 128 : (b + 1) * 384, :]
+        lines = jnp.concatenate([line[:, 256:]] * 4, axis=0)
+        wanted = lax.broadcasted_iota(jnp.int32, (32, 256), 0) + 64
+        hot_out[b * 256 : (b + 1) * 256, :] = jnp.where(lines == wanted, 1.0, 0.0).T.astype(BF16)
 
     def chunk(i, _):
         lanes = pl.ds(pl.multiple_of(i * 128, 128), 128)
@@ -266,7 +276,7 @@
         c.wait_send()
 
 
-def hyena(ids8, hit, emb4, gain, in_proj, short, taps, skip, wh):
+def hyena(ids, order, emb, gain, in_proj, short, taps, skip, wh):
     dma = pltpu.SemaphoreType.DMA
     vmem = pl.BlockSpec(memory_space=pltpu.VMEM)
     return pl.pallas_call(
@@ -276,9 +286,12 @@
             jax.ShapeDtypeStruct((512, 32), BF16),
             jax.ShapeDtypeStruct((2048, 4096), BF16),
         ),
-        in_specs=[vmem, pl.BlockSpec(memory_space=pltpu.SMEM), vmem, vmem, ANY, vmem, vmem, vmem, ANY],
+        in_specs=[vmem, pl.BlockSpec(memory_space=pltpu.SMEM), vmem, ANY, ANY, ANY, vmem, ANY, ANY],
         out_specs=(vmem, vmem, ANY),
         scratch_shapes=[
+            pltpu.VMEM(gain.shape, F32),
+            pltpu.VMEM(short.shape, F32),
+            pltpu.VMEM(skip.shape, F32),
             pltpu.VMEM((64, 8, 128), jnp.int32),
             pltpu.VMEM((3, 16, 2048), F32),
             pltpu.VMEM((128, 256), F32),
@@ -286,13 +299,13 @@
             pltpu.VMEM(in_proj.shape, BF16),
             pltpu.VMEM(wh.shape, BF16),
             dma((N_SENDS,)), dma((48,)), dma((2,)),
-            dma((9,)), dma((9,)), dma((3,)), dma((3,)), dma((3,)), dma((3,)), dma((3,)),
+            dma((9,)), dma((9,)), dma((3,)), dma((3,)), dma((3,)), dma((3,)), dma((3,)), dma((3,)),
         ],
         compiler_params=pltpu.CompilerParams(
             collective_id=0, has_side_effects=True, vmem_limit_bytes=48 * 2**20
         ),
         name="hyena",
-    )(ids8, hit, emb4, gain, in_proj, short, taps, skip, wh)
+    )(ids, order, emb, gain, in_proj, short, taps, skip, wh)
 
 
 def ab_of(dp, y, x):
@@ -531,12 +544,19 @@
                 o_ref[4 * (j + tile) + n] = out[n * 64 : (n + 1) * 64]
 
 
-def attend_return_kernel(slot_ref, q_ref, kv_ref, att_out, o_pos, o_ref, send, recv, loc):
+def attend_return_kernel(slot_ref, q_hbm, kv_hbm, att_out, q_ref, kv_ref, o_pos, o_ref, send, recv, loc, kv_sem):
     dp, y, x, t = coords()
     ctx = y * 4 + x
     a, b = ab_of(dp, y, x)
     barrier = pltpu.get_barrier_semaphore()
 
+    loads = [
+        pltpu.make_async_copy(kv_hbm, kv_ref, kv_sem.at[0]),
+        pltpu.make_async_copy(q_hbm, q_ref, kv_sem.at[1]),
+    ]
+    for c in loads:
+        c.start()
+
     def source(n):
         st, sa, r = n // 8, (n // 2) % 4, n % 2
         return st, ctx_of(dp, sa, 2 * (t % 2) + r)
@@ -554,6 +574,8 @@
         return 0
 
     lax.fori_loop(0, 32, hello, 0)
+    for c in loads:
+        c.wait()
     attend_kernel(slot_ref, q_ref, kv_ref, o_pos)
     for slot in range(32):
         o_ref[slot] = o_pos[slot_ref[33 + slot]]
@@ -608,37 +630,62 @@
 
 def attend_return(slots, q_all, kv_all):
     dma = pltpu.SemaphoreType.DMA
-    vmem = pl.BlockSpec(memory_space=pltpu.VMEM)
     return pl.pallas_call(
         attend_return_kernel,
         out_shape=jax.ShapeDtypeStruct((32, 64, 128), BF16),
-        in_specs=[pl.BlockSpec(memory_space=pltpu.SMEM), vmem, vmem],
+        in_specs=[pl.BlockSpec(memory_space=pltpu.SMEM), ANY, ANY],
         out_specs=ANY,
         scratch_shapes=[
-            pltpu.VMEM((32, 64, 128), BF16), pltpu.VMEM((32, 64, 128), BF16), dma((32,)), dma((32,)), dma
+            pltpu.VMEM(q_all.shape, BF16), pltpu.VMEM(kv_all.shape, BF16),
+            pltpu.VMEM((32, 64, 128), BF16), pltpu.VMEM((32, 64, 128), BF16), dma((32,)), dma((32,)), dma, dma((2,))
         ],
         compiler_params=pltpu.CompilerParams(
-            collective_id=2, has_side_effects=True, vmem_limit_bytes=48 * 2**20
+            collective_id=2, has_side_effects=True, vmem_limit_bytes=58 * 2**20
         ),
         name="attend_return",
     )(slots, q_all, kv_all)
+
+
+def final_kernel(att_ref, wa_ref, own_ref, out_ref):
+    rows = jnp.concatenate([att_ref[0], att_ref[1]], axis=1)
+
+    @pl.when(pl.program_id(0) == 0)
+    def _():
+        out_ref[...] = own_ref[...]
+
+    out_ref[...] += jnp.dot(rows, wa_ref[...], preferred_element_type=F32)
+
+
+def final(att, wa, own):
+    return pl.pallas_call(
+        final_kernel,
+        out_shape=jax.ShapeDtypeStruct((128, 4096), F32),
+        grid=(8,),
+        in_specs=[
+            pl.BlockSpec((2, 128, 128), lambda i: (i, 0, 0)),
+            pl.BlockSpec((256, 4096), lambda i: (i, 0)),
+            pl.BlockSpec((128, 4096), lambda i: (0, 0)),
+        ],
+        out_specs=pl.BlockSpec((128, 4096), lambda i: (0, 0)),
+        compiler_params=pltpu.CompilerParams(vmem_limit_bytes=58 * 2**20),
+        name="final",
+    )(att, wa, own)
 
 
 def body(ids, block_order, embed, mix_gain, in_proj, short_filter, long_filter, conv_skip,
          hyena_out, attn_gain, qkv_proj, attn_out):
     dp, y, x, t = coords()
     ctx = y * 4 + x
-    emb4 = jnp.concatenate([embed[c : c + 1] for c in CODES] + [jnp.zeros((28, embed.shape[1]), BF16)], axis=0)
+    emb32 = lax.slice_in_dim(embed, 64, 96, axis=0)
     taps = jnp.concatenate(
         [jnp.zeros((32, 1), F32), long_filter[:, ::-1], jnp.zeros((32, 127), F32)], axis=1
     )
     slot_ids = jnp.arange(32, dtype=jnp.int32)
     pair = 2 * ctx + jnp.arange(2, dtype=jnp.int32)
     owned = jnp.sum(jnp.where(slot_ids[None] == pair[:, None], block_order[None], 0), axis=1)
-    hit = (block_order[None, :] == owned[:, None] - 1).astype(jnp.int32).reshape(64)
-    ids8 = jnp.broadcast_to(ids.reshape(1, 128), (8, 128))
     mix, code_hot, wh = hyena(
-        ids8, hit, emb4, mix_gain.reshape(1, -1), in_proj, short_filter, taps, conv_skip.reshape(1, -1), hyena_out
+        ids.reshape(1, 128), block_order, emb32, mix_gain.reshape(1, -1), in_proj, short_filter, taps,
+        conv_skip.reshape(1, -1), hyena_out
     )
     wa = lax.all_gather(
         lax.dynamic_slice_in_dim(attn_out, (dp * 16 + ctx) * 16, 16, 0), ("tensor", "dp", "context"), axis=0, tiled=True
@@ -651,14 +698,13 @@
     cos = jnp.concatenate([cos, cos], axis=1)
     sin = jnp.concatenate([-sin, sin], axis=1)
     stream_own, q_all, kv_all = stream_qkv(
-        mix, wh, code_hot, emb4, attn_gain.reshape(1, -1), qkv_proj, cos, sin
+        mix, wh, code_hot, emb32, attn_gain.reshape(1, -1), qkv_proj, cos, sin
     )
     slot_of = jnp.sum(jnp.where(block_order[None, :] == slot_ids[:, None], slot_ids[None, :], 0), axis=1)
     _, b = ab_of(dp, y, x)
     slots = jnp.concatenate([slot_of, b.astype(jnp.int32).reshape(1), block_order])
     att = attend_return(slots, q_all, kv_all.reshape(16, 2, 2, 256, 128))
-    att = att.reshape(16, 128, 128).transpose(1, 0, 2).reshape(128, 2048)
-    return stream_own + jnp.dot(att, wa, preferred_element_type=F32)
+    return final(att.reshape(16, 128, 128), wa, stream_own)
 
 
 def solution(mesh):

time: 174 us -> 178 us (1.023)
  Pallas kernels: 137 us -> 151 us
  matrix products: 9.53 us -> 0 us
    pallas_call x0 -> x1, Pallas kernels: none -> 11.5 us  [final(): pl.pallas_call(final_kernel, out_shape=jax.ShapeDtypeStruct((128, 4096),...]
    dot_general x1 -> x0, matrix products: 9.53 us -> none  [body(): return stream_own + jnp.dot(att, wa, preferred_element_type=F32)]
    pallas_call x1, Pallas kernels: 50 us -> 52.6 us  [stream_qkv(): pl.pallas_call(proj_kernel, out_shape=(jax.ShapeDtypeStruct((128, 4096),...]
    unnamed x13 -> x17, local copies, waits for them, and re-layouts: 4.35 us -> 5.58 us
  transfers between devices with their start and end apart: 1 -> 1, of which waited for: 0 -> 0; matrix products, arithmetic and copies ran while one was open for 4% -> 3% of each run, Pallas kernels for 79% -> 79%
where the time goes in v5:
time: 178 us; the launch traced here: 177 us
  Pallas kernels  151 us (85%)
  between operations  13.5 us (8%)
  local copies, waits for them, and re-layouts  8.99 us (5%)
  other arithmetic  2.92 us (2%)
    pallas_call x1, Pallas kernels, hyena(): pl.pallas_call(hyena_kernel, out_shape=(jax.ShapeDtypeStruct((512, 2048),...  56.4 us
    pallas_call x1, Pallas kernels, stream_qkv(): pl.pallas_call(proj_kernel, out_shape=(jax.ShapeDtypeStruct((128, 4096),...  52.6 us
    pallas_call x1, Pallas kernels, attend_return(): pl.pallas_call(attend_return_kernel, out_shape=jax.ShapeDtypeStruct((32,...  31 us
    pallas_call x1, Pallas kernels, final(): pl.pallas_call(final_kernel, out_shape=jax.ShapeDtypeStruct((128, 4096),...  11.5 us
    unnamed x17, local copies, waits for them, and re-layouts  5.58 us
  transfers between devices with their start and end apart: 1, of which 0 were waited for; matrix products, arithmetic and copies ran while one was open for 3% of the time, Pallas kernels for 79%

profile of v5, /device:TPU:1, one launch (start us, length us, event | category | flops | bytes accessed | tf_op | source)
XLA Modules:
  0.0 176.9 jit_solution(10328884224434343260)
XLA Ops:
  6.5 0.0 all-gather.2.cloned.1.call-start
  6.5 1.6 constant_dynamic-slice_fusion
  8.1 0.0 all-gather.2.cloned.1.call-update
  8.1 1.0 slice.3.emb_ref
  9.1 0.8 rev.3
  9.9 0.1 pad.6.clone
  10.0 0.8 fusion.1
  10.8 0.1 convert_bitcast_fusion
  10.9 0.1 maximum_maximum_fusion.taps_ref
  11.0 0.0 copy-start.2
  11.0 0.7 copy-done.2
  11.7 0.0 copy-start.4
  11.7 0.7 copy-done.4
  12.5 0.0 copy-start.5
  12.5 0.7 copy-done.5
  13.1 0.0 copy-start.6
  13.1 0.7 copy-done.6
  13.8 0.0 copy-start.7
  13.8 0.7 copy-done.7
  14.4 0.0 copy-start.3
  14.4 56.4 %hyena.1 = (bf16[512,2048]{1,0:T(8,128)(2,1)S(1)}, bf16[512,32]{1,0:T(8,128)(2,1)S(1)}, bf16[2048,4096]{1,0:T(8,128)(2,1)}) custom-call(s32[1,128]{1,0:T(1,128)S(1)} %bitcast.14, s32[32]{0:T(128)S(1)} %copy-done.6, bf16[32,4096]{1,0:T(8,128)(2,1)S(1)} %slice.3.emb_ref, f32[1,4096]{1,0:T(1,128)S(1)} %bitcast.12, bf16[3,4096,512]{2,1,0:T(8,128)(2,1)} %proj_ref.1, ...), custom_call_target="tpu_custom_call" | custom-call | tf_op jit(solution)/shard_map/hyena/pallas_call | solution.py:282
  70.9 1.0 fusion
  71.9 0.2 pad_maximum_fusion
  72.1 0.0 copy-done.3
  72.1 52.6 %stream_qkv.1 = (f32[128,4096]{1,0:T(8,128)S(1)}, bf16[16,2,64,128]{3,2,1,0:T(8,128)(2,1)S(1)}, bf16[16,2,2,4,64,128]{5,4,3,2,1,0:T(8,128)(2,1)}) custom-call(bf16[512,2048]{1,0:T(8,128)(2,1)S(1)} %get-tuple-element.11.mix_ref, bf16[2048,4096]{1,0:T(8,128)(2,1)} %get-tuple-element.12.wh_ref, bf16[512,32]{1,0:T(8,128)(2,1)S(1)} %get-tuple-element.13.code_ref, ...), custom_call_target="tpu_custom_call" | custom-call | tf_op jit(solution)/shard_map/stream_qkv/pallas_call | solution.py:463
  124.7 0.0 copy-start
  124.7 1.3 copy-done
  126.0 0.0 copy-start.1
  126.0 0.8 copy-done.1
  126.8 0.1 select_reduce_fusion
  126.9 0.6 pad_add_fusion.slot_ref
  127.5 31.0 %attend_return.1 = bf16[32,64,128]{2,1,0:T(8,128)(2,1)} custom-call(s32[65]{0:T(128)} %pad_add_fusion.slot_ref, bf16[16,2,64,128]{3,2,1,0:T(8,128)(2,1)} %copy-done.1, bf16[16,2,2,256,128]{4,3,2,1,0:T(8,128)(2,1)} %bitcast.15), custom_call_target="tpu_custom_call" | custom-call | tf_op jit(solution)/shard_map/attend_return/pallas_call | solution.py:633
  158.5 0.0 all-gather.2.cloned.1.call-done.wa_ref
  158.5 11.5 %final.1 = f32[128,4096]{1,0:T(8,128)} custom-call(bf16[16,128,128]{2,1,0:T(8,128)(2,1)} %bitcast.16, bf16[2048,4096]{1,0:T(8,128)(2,1)} %all-gather.2.cloned.1.call-done.wa_ref, f32[128,4096]{1,0:T(8,128)} %copy-done), custom_call_target="tpu_custom_call" | custom-call | tf_op jit(solution)/shard_map/final/pallas_call | solution.py:660
  (6 shorter events, 0.0 us)
Async XLA Ops:
  6.5 152.0 %all-gather.2.cloned.1.call-start = ((), (), s32[]{:S(2)}) async-start(), calls=%async_computation | async-start | bytes 16908288 | tf_op jit(solution)/shard_map/all_gather | solution.py:690
  11.0 0.7 copy-start.2
  11.7 0.7 copy-start.4
  12.5 0.7 copy-start.5
  13.1 0.7 copy-start.6
  13.8 0.7 copy-start.7
  14.4 57.6 %copy-start.3 = (f32[4096]{0:T(1024)S(1)}, f32[4096]{0:T(1024)}, u32[]{:S(2)}) copy-start(f32[4096]{0:T(1024)} %param.21) | copy-start | bytes 49156
  124.7 1.3 copy-start
  126.0 0.8 copy-start.1
Sparse Core Ops, SparseCore 0:
  10.5 89.8 all-gather.1

commit v6 on v5

--- a/solution.py
+++ b/solution.py
@@ -544,18 +544,15 @@
                 o_ref[4 * (j + tile) + n] = out[n * 64 : (n + 1) * 64]
 
 
-def attend_return_kernel(slot_ref, q_hbm, kv_hbm, att_out, q_ref, kv_ref, o_pos, o_ref, send, recv, loc, kv_sem):
+def attend_return_kernel(slot_ref, q_ref, kv_ref, wa_hbm, own_ref, out_ref, att_out, wa_ref, rows_ref, o_pos, o_ref,
+                         send, recv, loc, wa_sem):
     dp, y, x, t = coords()
     ctx = y * 4 + x
     a, b = ab_of(dp, y, x)
     barrier = pltpu.get_barrier_semaphore()
 
-    loads = [
-        pltpu.make_async_copy(kv_hbm, kv_ref, kv_sem.at[0]),
-        pltpu.make_async_copy(q_hbm, q_ref, kv_sem.at[1]),
-    ]
-    for c in loads:
-        c.start()
+    wa_load = pltpu.make_async_copy(wa_hbm, wa_ref, wa_sem)
+    wa_load.start()
 
     def source(n):
         st, sa, r = n // 8, (n // 2) % 4, n % 2
@@ -574,8 +571,6 @@
         return 0
 
     lax.fori_loop(0, 32, hello, 0)
-    for c in loads:
-        c.wait()
     attend_kernel(slot_ref, q_ref, kv_ref, o_pos)
     for slot in range(32):
         o_ref[slot] = o_pos[slot_ref[33 + slot]]
@@ -626,50 +621,36 @@
         return 0
 
     lax.fori_loop(0, 32, finish, 0)
-
-
-def attend_return(slots, q_all, kv_all):
+    wa_load.wait()
+    for head in range(16):
+        for r in range(2):
+            rows_ref[r * 64 : (r + 1) * 64, head * 128 : (head + 1) * 128] = att_out[2 * head + r]
+
+    def tile(n, _):
+        lanes = pl.ds(pl.multiple_of(n * 512, 512), 512)
+        out_ref[:, lanes] = own_ref[:, lanes] + jnp.dot(rows_ref[...], wa_ref[:, lanes], preferred_element_type=F32)
+        return 0
+
+    lax.fori_loop(0, 8, tile, 0)
+
+
+def attend_return(slots, q_all, kv_all, wa, own):
     dma = pltpu.SemaphoreType.DMA
+    vmem = pl.BlockSpec(memory_space=pltpu.VMEM)
     return pl.pallas_call(
         attend_return_kernel,
-        out_shape=jax.ShapeDtypeStruct((32, 64, 128), BF16),
-        in_specs=[pl.BlockSpec(memory_space=pltpu.SMEM), ANY, ANY],
-        out_specs=ANY,
+        out_shape=jax.ShapeDtypeStruct((128, 4096), F32),
+        in_specs=[pl.BlockSpec(memory_space=pltpu.SMEM), vmem, vmem, ANY, vmem],
+        out_specs=vmem,
         scratch_shapes=[
-            pltpu.VMEM(q_all.shape, BF16), pltpu.VMEM(kv_all.shape, BF16),
-            pltpu.VMEM((32, 64, 128), BF16), pltpu.VMEM((32, 64, 128), BF16), dma((32,)), dma((32,)), dma, dma((2,))
+            pltpu.VMEM((32, 64, 128), BF16), pltpu.VMEM(wa.shape, BF16), pltpu.VMEM((128, 2048), BF16),
+            pltpu.VMEM((32, 64, 128), BF16), pltpu.VMEM((32, 64, 128), BF16), dma((32,)), dma((32,)), dma, dma
         ],
         compiler_params=pltpu.CompilerParams(
-            collective_id=2, has_side_effects=True, vmem_limit_bytes=58 * 2**20
+            collective_id=2, has_side_effects=True, vmem_limit_bytes=48 * 2**20
         ),
         name="attend_return",
-    )(slots, q_all, kv_all)
-
-
-def final_kernel(att_ref, wa_ref, own_ref, out_ref):
-    rows = jnp.concatenate([att_ref[0], att_ref[1]], axis=1)
-
-    @pl.when(pl.program_id(0) == 0)
-    def _():
-        out_ref[...] = own_ref[...]
-
-    out_ref[...] += jnp.dot(rows, wa_ref[...], preferred_element_type=F32)
-
-
-def final(att, wa, own):
-    return pl.pallas_call(
-        final_kernel,
-        out_shape=jax.ShapeDtypeStruct((128, 4096), F32),
-        grid=(8,),
-        in_specs=[
-            pl.BlockSpec((2, 128, 128), lambda i: (i, 0, 0)),
-            pl.BlockSpec((256, 4096), lambda i: (i, 0)),
-            pl.BlockSpec((128, 4096), lambda i: (0, 0)),
-        ],
-        out_specs=pl.BlockSpec((128, 4096), lambda i: (0, 0)),
-        compiler_params=pltpu.CompilerParams(vmem_limit_bytes=58 * 2**20),
-        name="final",
-    )(att, wa, own)
+    )(slots, q_all, kv_all, wa, own)
 
 
 def body(ids, block_order, embed, mix_gain, in_proj, short_filter, long_filter, conv_skip,
@@ -700,11 +681,11 @@
     stream_own, q_all, kv_all = stream_qkv(
         mix, wh, code_hot, emb32, attn_gain.reshape(1, -1), qkv_proj, cos, sin
     )
+    wa, kv_all = lax.optimization_barrier((wa, kv_all))
     slot_of = jnp.sum(jnp.where(block_order[None, :] == slot_ids[:, None], slot_ids[None, :], 0), axis=1)
     _, b = ab_of(dp, y, x)
     slots = jnp.concatenate([slot_of, b.astype(jnp.int32).reshape(1), block_order])
-    att = attend_return(slots, q_all, kv_all.reshape(16, 2, 2, 256, 128))
-    return final(att.reshape(16, 128, 128), wa, stream_own)
+    return attend_return(slots, q_all, kv_all.reshape(16, 2, 2, 256, 128), wa, stream_own)
 
 
 def solution(mesh):

time: 178 us -> 169 us (0.949)
  Pallas kernels: 151 us -> 144 us
    pallas_call x2 -> x1, Pallas kernels: 42.5 us -> 35.2 us  [attend_return(): pl.pallas_call(attend_return_kernel, out_shape=jax.ShapeDtypeStruct((128,...]
    unnamed x17 -> x16, local copies, waits for them, and re-layouts: 5.58 us -> 4.79 us
  transfers between devices with their start and end apart: 1 -> 1, of which waited for: 0 -> 0; matrix products, arithmetic and copies ran while one was open for 3% -> 3% of each run, Pallas kernels for 79% -> 65%
where the time goes in v6:
time: 169 us; the launch traced here: 168 us
  Pallas kernels  144 us (85%)
  between operations  13.5 us (8%)
  local copies, waits for them, and re-layouts  8.2 us (5%)
  other arithmetic  2.4 us (1%)
    pallas_call x1, Pallas kernels, hyena(): pl.pallas_call(hyena_kernel, out_shape=(jax.ShapeDtypeStruct((512, 2048),...  56.4 us
    pallas_call x1, Pallas kernels, stream_qkv(): pl.pallas_call(proj_kernel, out_shape=(jax.ShapeDtypeStruct((128, 4096),...  52.6 us
    pallas_call x1, Pallas kernels, attend_return(): pl.pallas_call(attend_return_kernel, out_shape=jax.ShapeDtypeStruct((128,...  35.2 us
    unnamed x16, local copies, waits for them, and re-layouts  4.79 us
  transfers between devices with their start and end apart: 1, of which 0 were waited for; matrix products, arithmetic and copies ran while one was open for 3% of the time, Pallas kernels for 65%

profile of v6, /device:TPU:1, one launch (start us, length us, event | category | flops | bytes accessed | tf_op | source)
XLA Modules:
  0.0 168.3 jit_solution(2311939399198355760)
XLA Ops:
  6.5 0.0 all-gather.2.cloned.1.call-start
  6.5 1.6 constant_dynamic-slice_fusion
  8.1 0.0 all-gather.2.cloned.1.call-update
  8.1 1.0 slice.3.emb_ref
  9.1 0.8 rev.3
  9.9 0.1 pad.6.clone
  10.0 0.8 fusion.1
  10.8 0.1 convert_bitcast_fusion
  10.9 0.1 maximum_maximum_fusion.taps_ref
  11.0 0.0 copy-start
  11.0 0.7 copy-done
  11.7 0.0 copy-start.2
  11.7 0.7 copy-done.2
  12.5 0.0 copy-start.3
  12.5 0.7 copy-done.3
  13.1 0.0 copy-start.4
  13.1 0.7 copy-done.4
  13.8 0.0 copy-start.6
  13.8 0.7 copy-done.6
  14.4 0.0 copy-start.1
  14.4 56.4 %hyena.1 = (bf16[512,2048]{1,0:T(8,128)(2,1)S(1)}, bf16[512,32]{1,0:T(8,128)(2,1)S(1)}, bf16[2048,4096]{1,0:T(8,128)(2,1)}) custom-call(s32[1,128]{1,0:T(1,128)S(1)} %bitcast.13, s32[32]{0:T(128)S(1)} %copy-done.4, bf16[32,4096]{1,0:T(8,128)(2,1)S(1)} %slice.3.emb_ref, f32[1,4096]{1,0:T(1,128)S(1)} %bitcast.11, bf16[3,4096,512]{2,1,0:T(8,128)(2,1)} %proj_ref.1, ...), custom_call_target="tpu_custom_call" | custom-call | tf_op jit(solution)/shard_map/hyena/pallas_call | solution.py:282
  70.9 1.0 fusion
  71.9 0.2 pad_maximum_fusion
  72.1 0.0 copy-done.1
  72.1 0.0 copy-start.5
  72.1 52.6 %stream_qkv.1 = (f32[128,4096]{1,0:T(8,128)S(1)}, bf16[16,2,64,128]{3,2,1,0:T(8,128)(2,1)S(1)}, bf16[16,2,2,4,64,128]{5,4,3,2,1,0:T(8,128)(2,1)}) custom-call(bf16[512,2048]{1,0:T(8,128)(2,1)S(1)} %get-tuple-element.13.mix_ref, bf16[2048,4096]{1,0:T(8,128)(2,1)} %get-tuple-element.14.wh_ref, bf16[512,32]{1,0:T(8,128)(2,1)S(1)} %get-tuple-element.15.code_ref, ...), custom_call_target="tpu_custom_call" | custom-call | tf_op jit(solution)/shard_map/stream_qkv/pallas_call | solution.py:463
  124.7 0.0 copy-done.5
  124.7 0.1 select_reduce_fusion
  124.8 0.1 pad_add_fusion.slot_ref
  124.9 0.0 all-gather.2.cloned.1.call-done.wa_hbm
  124.9 35.2 %attend_return.1 = f32[128,4096]{1,0:T(8,128)S(1)} custom-call(s32[65]{0:T(128)S(1)} %pad_add_fusion.slot_ref, bf16[16,2,64,128]{3,2,1,0:T(8,128)(2,1)S(1)} %get-tuple-element.16.q_ref, bf16[16,2,2,256,128]{4,3,2,1,0:T(8,128)(2,1)} %bitcast.14, bf16[2048,4096]{1,0:T(8,128)(2,1)} %all-gather.2.cloned.1.call-done.wa_hbm, f32[128,4096]{1,0:T(8,128)S(1)} %get-tuple-element.20.own_ref), custom_call_target="tpu_custom_call" | custom-call | tf_op jit(solution)/shard_map/attend_return/pallas_call | solution.py:640
  160.1 1.3 copy.15
  (6 shorter events, 0.0 us)
Async XLA Ops:
  6.5 118.4 %all-gather.2.cloned.1.call-start = ((), (), s32[]{:S(2)}) async-start(), calls=%async_computation | async-start | bytes 16908288 | tf_op jit(solution)/shard_map/all_gather | solution.py:671
  11.0 0.7 copy-start
  11.7 0.7 copy-start.2
  12.5 0.7 copy-start.3
  13.1 0.7 copy-start.4
  13.8 0.7 copy-start.6
  14.4 57.6 %copy-start.1 = (f32[4096]{0:T(1024)S(1)}, f32[4096]{0:T(1024)}, u32[]{:S(2)}) copy-start(f32[4096]{0:T(1024)} %param.21) | copy-start | bytes 49156
  72.1 52.6 %copy-start.5 = (s32[32]{0:T(128)S(1)}, s32[32]{0:T(128)}, u32[]{:S(2)}) copy-start(s32[32]{0:T(128)} %order_ref.1) | copy-start | bytes 388
Sparse Core Ops, SparseCore 0:
  10.5 89.9 all-gather.1
